TPU v7x, 256 devices: a whole 4x4x8 slice. The times are simulated.
256 devices in a mesh: head: 8 (over z_hi, core), frame: 32 (over z_lo, y, x).
Axes of the slice: x: 4, y: 4, z: 8 (z_hi: 4, z_lo: 2; z = z_hi * 2 + z_lo), core: 2. Of those that a mesh axis runs over, the one named last changes fastest.
Arguments:
- resid: bfloat16 [12288, 5120], P('frame'), may hold values from -6 to 6
- qkv: bfloat16 [12288, 3, 5120], P(('frame', 'head')), may hold values from -12 to 12
- band: int32 [32, 9], P('frame'), may hold values from 1 to 384, as said below
- out_weight: bfloat16 [5120, 5120], P('head'), may hold values from -0.078125 to 0.078125
- modulation: float32 [4, 5120], replicated, may hold values from -3 to 3
- up_weight: bfloat16 [5120, 6912], P('frame', 'head'), may hold values from -0.078125 to 0.078125
- down_weight: bfloat16 [6912, 5120], P('head', 'frame'), may hold values from -0.078125 to 0.078125
Outputs:
- mixed: bfloat16 [12288, 5120], P(('frame', 'head'))
Inputs may be any that keep to these rules, and one draw needn't show every extreme that they name: `band`: column 0 (the block itself) is 384; the column of a partner at distance d is at most 384 // d.
All inputs are finite; a program needn't handle non-finite values.
Results may differ from a plain program's by a relative error of at most 0.012.
Values may be sent and summed in bfloat16 or wider, within the bound.
A program may use at most 128 MiB of HBM per device.

v0:
```python
import math

import jax
import jax.numpy as jnp
from jax import lax
from jax.sharding import PartitionSpec as P

HD = 128
SLOTS = 9


partner_offsets = (0, -8, -4, -2, -1, 1, 2, 4, 8)


def shifted(block, axis, distance):
    devices = range(lax.axis_size(axis))
    route = [(i - distance, i) for i in devices if i - distance in devices]
    return lax.ppermute(block, axis, route)


def rounded(values):
    narrow = lax.optimization_barrier(values.astype(jnp.bfloat16))
    return narrow.astype(jnp.float32)


def modulate(residual_state, shift_row, scale_row):
    average = jnp.mean(residual_state, axis=-1, keepdims=True)
    centered = residual_state - average
    variance = jnp.mean(centered * centered, axis=-1, keepdims=True)
    normal_form = centered * lax.rsqrt(variance + 1e-06)
    return (normal_form * (1.0 + scale_row) + shift_row).astype(jnp.bfloat16)


def shards(resid, qkv, band, out_weight, modulation, up_weight, down_weight):
    head_count = lax.axis_size("head")
    frame_count = lax.axis_size("frame")
    frame_index = lax.axis_index("frame")
    head_index = lax.axis_index("head")
    gathered_heads = lax.all_to_all(qkv, "head", split_axis=2, concat_axis=0, tiled=True)
    block_len = gathered_heads.shape[0]
    inner_dev = gathered_heads.shape[2]
    head_group = inner_dev // HD
    queries = gathered_heads[:, 0].reshape(block_len, head_group, HD)
    key_value = gathered_heads[:, 1:]
    neighbours = [key_value]
    for offset in partner_offsets[1:]:
        neighbours.append(shifted(key_value, "frame", -offset))
    stacked = jnp.stack(neighbours, 0)
    key_rows = stacked[:, :, 0].reshape(SLOTS, block_len, head_group, HD)
    value_rows = stacked[:, :, 1].reshape(SLOTS, block_len, head_group, HD)
    offsets = jnp.array(partner_offsets, jnp.int32)
    partner = frame_index + offsets
    present = (partner >= 0) & (partner < frame_count)
    widths = band[0]
    positions = jnp.arange(block_len, dtype=jnp.int32)
    distance = jnp.abs(positions[:, None] - positions[None, :])
    allowed = (distance[None, :, :] < widths[:, None, None]) & present[:, None, None]
    allowed = jnp.transpose(allowed, (1, 0, 2))[None]
    score_scale = 1.0 / math.sqrt(HD)
    scores = (
        jnp.einsum("igd,sjgd->gisj", queries, key_rows, preferred_element_type=jnp.float32)
        * score_scale
    )
    masked = jnp.where(allowed, scores, -1e30)
    row_max = jnp.max(masked, axis=(2, 3), keepdims=True)
    weights = jnp.where(allowed, jnp.exp(masked - row_max), 0.0)
    denominator = jnp.sum(weights, axis=(2, 3))
    probabilities = weights.astype(jnp.bfloat16)
    summed = jnp.einsum(
        "gisj,sjgd->igd", probabilities, value_rows, preferred_element_type=jnp.float32
    )
    attended = (
        (summed / jnp.transpose(denominator)[:, :, None])
        .astype(jnp.bfloat16)
        .reshape(block_len, inner_dev)
    )
    partial_value = rounded(jnp.dot(attended, out_weight, preferred_element_type=jnp.float32))
    rows_dev = block_len // head_count
    first_row = head_index * rows_dev
    branch = lax.psum(partial_value.astype(jnp.bfloat16), "head").astype(jnp.float32)
    residual_state = resid.astype(jnp.float32) + modulation[0] * branch
    normed = modulate(residual_state, modulation[1], modulation[2])
    state_rows = lax.dynamic_slice_in_dim(residual_state, first_row, rows_dev, 0)
    projected = jnp.dot(
        normed,
        lax.all_gather(up_weight, "frame", axis=0, tiled=True),
        preferred_element_type=jnp.float32,
    )
    hidden = jax.nn.gelu(projected, approximate=True).astype(jnp.bfloat16)
    down_terms = rounded(
        jnp.dot(
            hidden,
            lax.all_gather(down_weight, "frame", axis=1, tiled=True),
            preferred_element_type=jnp.float32,
        )
    )
    ffn_out = lax.psum_scatter(
        down_terms.astype(jnp.bfloat16), "head", scatter_dimension=0, tiled=True
    ).astype(jnp.float32)
    return (state_rows + modulation[3] * ffn_out).astype(jnp.bfloat16)


def solution(mesh):
    in_specs = (
        P("frame", None),
        P(("frame", "head"), None, None),
        P("frame", None),
        P("head", None),
        P(),
        P("frame", "head"),
        P("head", "frame"),
    )
    out_specs = P(("frame", "head"), None)
    return jax.shard_map(shards, mesh=mesh, in_specs=in_specs, out_specs=out_specs, check_vma=False)
```

profile of v0, /device:TPU:32, one launch (start us, length us, event | category | flops | bytes accessed | tf_op | source)
XLA Modules:
  0.0 785.9 jit_solution(9519063999046773467)
XLA Ops:
  7.4 7.2 copy.24
  14.5 8.9 %reshape.37 = bf16[8,2,46080]{2,1,0:T(2,128)(2,1)} reshape(bf16[5120,3,48]{2,1,0:T(4,128)(2,1)} %bitcast.62) | data formatting | bytes 2949120
  23.4 7.6 all-to-all-start
  31.0 38.3 %all-to-all-done = bf16[8,2,46080]{2,1,0:T(2,128)(2,1)S(1)} async-done(((bf16[8,2,46080]{2,1,0:T(2,128)(2,1)}), bf16[8,2,46080]{2,1,0:T(2,128)(2,1)S(1)}, u32[]{:S(2)}, u32[]{:S(2)}) %all-to-all-start) | async-done | bytes 1474592 | tf_op jit(solution)/shard_map/all_to_all | solution.py:39
  69.4 7.6 reshape.38
  77.0 5.9 copy.37
  83.9 5.1 collective-permute-start
  89.1 2.6 collective-permute-start.1
  91.7 4.9 collective-permute-start.2
  97.6 2.5 collective-permute-start.3
  100.1 7.6 collective-permute-start.4
  108.8 45.4 %collective-permute-done = bf16[384,2,640]{2,0,1:T(8,128)(2,1)} collective-permute-done((bf16[384,2,640]{2,0,1:T(8,128)(2,1)}, bf16[384,2,640]{2,0,1:T(8,128)(2,1)}, u32[]{:S(2)}, u32[]{:S(2)}) %collective-permute-start) | collective-permute-done | bytes 983072 | tf_op jit(solution)/shard_map/ppermute | solution.py:18
  157.5 16.6 %collective-permute-done.1 = bf16[384,2,640]{2,0,1:T(8,128)(2,1)} collective-permute-done((bf16[384,2,640]{2,0,1:T(8,128)(2,1)}, bf16[384,2,640]{2,0,1:T(8,128)(2,1)}, u32[]{:S(2)}, u32[]{:S(2)}) %collective-permute-start.1) | collective-permute-done | bytes 983072 | tf_op jit(solution)/shard_map/ppermute | solution.py:18
  177.4 2.1 collective-permute-start.7
  180.9 10.9 %collective-permute-done.3 = bf16[384,2,640]{2,0,1:T(8,128)(2,1)} collective-permute-done((bf16[384,2,640]{2,0,1:T(8,128)(2,1)}, bf16[384,2,640]{2,0,1:T(8,128)(2,1)}, u32[]{:S(2)}, u32[]{:S(2)}) %collective-permute-start.3) | collective-permute-done | bytes 983072 | tf_op jit(solution)/shard_map/ppermute | solution.py:18
  195.1 31.0 %collective-permute-done.6 = bf16[384,2,640]{2,0,1:T(8,128)(2,1)S(1)} collective-permute-done((bf16[384,2,640]{2,0,1:T(8,128)(2,1)}, bf16[384,2,640]{2,0,1:T(8,128)(2,1)S(1)}, u32[]{:S(2)}, u32[]{:S(2)}) %collective-permute-start.6) | collective-permute-done | bytes 983072 | tf_op jit(solution)/shard_map/ppermute | solution.py:18
  226.2 17.9 %collective-permute-done.7 = bf16[384,2,640]{2,0,1:T(8,128)(2,1)S(1)} collective-permute-done((bf16[384,2,640]{2,0,1:T(8,128)(2,1)}, bf16[384,2,640]{2,0,1:T(8,128)(2,1)S(1)}, u32[]{:S(2)}, u32[]{:S(2)}) %collective-permute-start.7) | collective-permute-done | bytes 983072 | tf_op jit(solution)/shard_map/ppermute | solution.py:18
  244.3 4.1 fusion.30
  248.4 8.0 %copy.28 = bf16[9,384,1,640]{1,3,0,2:T(8,128)(2,1)} copy(bf16[9,384,1,640]{3,1,2,0:T(8,128)(2,1)} %get-tuple-element.9) | data formatting | bytes 8847360 | tf_op jit(solution)/shard_map/slice | solution.py:49
  256.4 8.0 %copy.27 = bf16[9,384,1,640]{1,3,0,2:T(8,128)(2,1)} copy(bf16[9,384,1,640]{3,1,2,0:T(8,128)(2,1)} %get-tuple-element.10) | data formatting | bytes 8847360 | tf_op jit(solution)/shard_map/slice | solution.py:50
  264.4 14.2 %fusion = (f32[5,384]{1,0:T(8,128)S(1)}, f32[5,9,384,384]{3,2,1,0:T(8,128)}) fusion(pred[384,9,384]{0,2,1:T(8,128)(4,1)S(1)} %compare_and_fusion, bf16[384,5,128,1]{0,2,3,1:T(8,128)(2,1)S(1)} %bitcast.69, bf16[9,384,5,128]{1,3,2,0:T(8,128)(2,1)} %bitcast.67), kind=kOutput, calls=%fused_computation.2 | convolution fusion | flops 1718597760 | bytes 32792064 | tf_op jit(solution)/shard_map/igd,sjgd->gisj/dot_general | solution.py:61
  278.6 12.5 %fusion.1 = (f32[5,384]{1,0:T(8,128)S(1)}, bf16[5,384,9,384]{1,3,2,0:T(8,128)(2,1)S(1)}) fusion(f32[5,9,384,384]{3,2,1,0:T(8,128)} %get-tuple-element.16, f32[5,384]{1,0:T(8,128)S(1)} %get-tuple-element.15, pred[384,9,384]{0,2,1:T(8,128)(4,1)S(1)} %compare_and_fusion), kind=kLoop, calls=%fused_computation.3 | loop fusion | flops 39811200 | bytes 41155584 | tf_op jit(solution)/shard_map/reduce_sum | solution.py:67
  291.1 5.0 divide_convert_fusion
  296.1 8.1 %convolution_convert_fusion = bf16[384,5120]{1,0:T(8,128)(2,1)} fusion(bf16[384,640]{0,1:T(8,128)(2,1)S(1)} %bitcast.68, bf16[640,5120]{1,0:T(8,128)(2,1)} %param.11), kind=kOutput, calls=%fused_computation.10 | convolution fusion | flops 2518548480 | bytes 10977280 | tf_op jit(solution)/shard_map/dot_general | solution.py:77
  305.7 140.1 %all-reduce.2.cloned.1.call-done = bf16[384,5120]{1,0:T(8,128)(2,1)} async-done(((bf16[384,5120]{1,0:T(8,128)(2,1)}), bf16[384,5120]{1,0:T(8,128)(2,1)}) %all-reduce.2.cloned.1.call-update) | async-done | bytes 3932176 | tf_op jit(solution)/shard_map/psum | solution.py:80
  445.8 4.8 fusion.29
  450.6 3.2 copy-done
  454.7 69.3 %all-gather.3.cloned.1.call-done = bf16[5120,864]{1,0:T(8,128)(2,1)} async-done(((bf16[160,864]{1,0:T(8,128)(2,1)}), bf16[5120,864]{1,0:T(8,128)(2,1)}) %all-gather.3.cloned.1.call-update) | async-done | bytes 8847376 | tf_op jit(solution)/shard_map/all_gather | solution.py:86
  524.0 172.2 %all-gather.5.cloned.1.call-done = bf16[864,5120]{0,1:T(8,128)(2,1)} async-done(((bf16[864,160]{0,1:T(8,128)(2,1)}), bf16[864,5120]{0,1:T(8,128)(2,1)}) %all-gather.5.cloned.1.call-update) | async-done | bytes 8847376 | tf_op jit(solution)/shard_map/all_gather | solution.py:93
  696.2 22.3 %convolution_convert_fusion.1 = bf16[384,5120]{1,0:T(8,128)(2,1)} fusion(bf16[864,5120]{0,1:T(8,128)(2,1)} %all-gather.5.cloned.1.call-done, bf16[5120,864]{1,0:T(8,128)(2,1)} %all-gather.3.cloned.1.call-done, f32[384,5120]{1,0:T(8,128)} %copy-done, f32[5120]{0:T(1024)S(1)} %bitcast.72, f32[5120]{0:T(1024)S(1)} %bitcast.73, f32[384]{0:T(512)S(1)} %add_rsqrt_fusion, ...), kind=kOutput, calls=%fused_computation.11 | convolution fusion | flops 6809554944 | bytes 29535232 | tf_op jit(solution)/shard_map/dot_general | solution.py:91
  718.5 57.7 %reduce-scatter.2.cloned.1.call-done = bf16[48,5120]{1,0:T(8,128)(2,1)} async-done(((bf16[384,5120]{1,0:T(8,128)(2,1)}), bf16[48,5120]{1,0:T(8,128)(2,1)}) %reduce-scatter.2.cloned.1.call-update) | async-done | bytes 491536 | tf_op jit(solution)/shard_map/reduce_scatter | solution.py:97
  776.2 2.2 add_convert_fusion.4
  (41 shorter events, 17.1 us)
Async XLA Ops:
  23.4 45.9 %all-to-all-start = ((bf16[8,2,46080]{2,1,0:T(2,128)(2,1)}), bf16[8,2,46080]{2,1,0:T(2,128)(2,1)S(1)}, u32[]{:S(2)}, u32[]{:S(2)}) async-start(bf16[8,2,46080]{2,1,0:T(2,128)(2,1)} %reshape.37), calls=%async_computation | async-start | bytes 2949120 | tf_op jit(solution)/shard_map/all_to_all | solution.py:39
  31.0 58.1 %copy-start.4 = (s32[9]{0:T(128)S(1)}, s32[9]{0:T(128)}, u32[]{:S(2)}) copy-start(s32[9]{0:T(128)} %constant.43.clone) | copy-start | bytes 112
  31.0 414.8 %all-reduce.2.cloned.1.call-start = ((), (), s32[]{:S(2)}) async-start(), calls=%async_computation.2 | async-start | bytes 7864320 | tf_op jit(solution)/shard_map/psum | solution.py:80
  31.0 65.6 %copy-start.3 = (s32[1,9]{1,0:T(1,128)S(1)}, s32[1,9]{1,0:T(1,128)}, u32[]{:S(2)}) copy-start(s32[1,9]{1,0:T(1,128)} %param.10) | copy-start | bytes 112
  83.9 70.3 %collective-permute-start = (bf16[384,2,640]{2,0,1:T(8,128)(2,1)}, bf16[384,2,640]{2,0,1:T(8,128)(2,1)}, u32[]{:S(2)}, u32[]{:S(2)}) collective-permute-start(bf16[384,2,640]{2,0,1:T(8,128)(2,1)} %slice.32), channel_id=1, source_target_pairs={{0,8},{1,9},{2,10},{3,11},{4,12},{5,13},{6,14},{7,15},{8,16},{9,17... | collective-permute-start | bytes 2949128 | tf_op jit(solution)/shard_map/ppermute | solution.py:18
  89.1 85.1 %collective-permute-start.1 = (bf16[384,2,640]{2,0,1:T(8,128)(2,1)}, bf16[384,2,640]{2,0,1:T(8,128)(2,1)}, u32[]{:S(2)}, u32[]{:S(2)}) collective-permute-start(bf16[384,2,640]{2,0,1:T(8,128)(2,1)} %slice.32), channel_id=1, source_target_pairs={{0,4},{1,5},{2,6},{3,7},{4,8},{5,9},{6,10},{7,11},{8,12},{9,13},{1... | collective-permute-start | bytes 2949128 | tf_op jit(solution)/shard_map/ppermute | solution.py:18
  91.7 85.7 %collective-permute-start.2 = (bf16[384,2,640]{2,0,1:T(8,128)(2,1)}, bf16[384,2,640]{2,0,1:T(8,128)(2,1)}, u32[]{:S(2)}, u32[]{:S(2)}) collective-permute-start(bf16[384,2,640]{2,0,1:T(8,128)(2,1)} %slice.32), channel_id=1, source_target_pairs={{0,2},{1,3},{2,4},{3,5},{4,6},{5,7},{6,8},{7,9},{8,10},{9,11},{10,... | collective-permute-start | bytes 2949128 | tf_op jit(solution)/shard_map/ppermute | solution.py:18
  97.6 94.2 %collective-permute-start.3 = (bf16[384,2,640]{2,0,1:T(8,128)(2,1)}, bf16[384,2,640]{2,0,1:T(8,128)(2,1)}, u32[]{:S(2)}, u32[]{:S(2)}) collective-permute-start(bf16[384,2,640]{2,0,1:T(8,128)(2,1)} %slice.32), channel_id=1, source_target_pairs={{0,1},{1,2},{2,3},{3,4},{4,5},{5,6},{6,7},{7,8},{8,9},{9,10},{10,1... | collective-permute-start | bytes 2949128 | tf_op jit(solution)/shard_map/ppermute | solution.py:18
  100.1 93.1 %collective-permute-start.4 = (bf16[384,2,640]{2,0,1:T(8,128)(2,1)}, bf16[384,2,640]{2,0,1:T(8,128)(2,1)}, u32[]{:S(2)}, u32[]{:S(2)}) collective-permute-start(bf16[384,2,640]{2,0,1:T(8,128)(2,1)} %slice.32), channel_id=1, source_target_pairs={{1,0},{2,1},{3,2},{4,3},{5,4},{6,5},{7,6},{8,7},{9,8},{10,9},{11,1... | collective-permute-start | bytes 2949128 | tf_op jit(solution)/shard_map/ppermute | solution.py:18
  154.2 40.7 %collective-permute-start.5 = (bf16[384,2,640]{2,0,1:T(8,128)(2,1)}, bf16[384,2,640]{2,0,1:T(8,128)(2,1)S(1)}, u32[]{:S(2)}, u32[]{:S(2)}) collective-permute-start(bf16[384,2,640]{2,0,1:T(8,128)(2,1)} %slice.32), channel_id=1, source_target_pairs={{2,0},{3,1},{4,2},{5,3},{6,4},{7,5},{8,6},{9,7},{10,8},{11,9},{12,... | collective-permute-start | bytes 2949128 | tf_op jit(solution)/shard_map/ppermute | solution.py:18
  174.1 51.9 %collective-permute-start.6 = (bf16[384,2,640]{2,0,1:T(8,128)(2,1)}, bf16[384,2,640]{2,0,1:T(8,128)(2,1)S(1)}, u32[]{:S(2)}, u32[]{:S(2)}) collective-permute-start(bf16[384,2,640]{2,0,1:T(8,128)(2,1)} %slice.32), channel_id=1, source_target_pairs={{4,0},{5,1},{6,2},{7,3},{8,4},{9,5},{10,6},{11,7},{12,8},{13,9},{1... | collective-permute-start | bytes 2949128 | tf_op jit(solution)/shard_map/ppermute | solution.py:18
  177.4 66.7 %collective-permute-start.7 = (bf16[384,2,640]{2,0,1:T(8,128)(2,1)}, bf16[384,2,640]{2,0,1:T(8,128)(2,1)S(1)}, u32[]{:S(2)}, u32[]{:S(2)}) collective-permute-start(bf16[384,2,640]{2,0,1:T(8,128)(2,1)} %slice.32), channel_id=1, source_target_pairs={{8,0},{9,1},{10,2},{11,3},{12,4},{13,5},{14,6},{15,7},{16,8},{17,9... | collective-permute-start | bytes 2949128 | tf_op jit(solution)/shard_map/ppermute | solution.py:18
  248.4 16.0 %copy-start.1 = (bf16[384,1,640]{0,2,1:T(8,128)(2,1)S(1)}, bf16[384,1,640]{0,2,1:T(8,128)(2,1)}, u32[]{:S(2)}) copy-start(bf16[384,1,640]{0,2,1:T(8,128)(2,1)} %copy.29) | copy-start | bytes 1474564
  296.0 9.6 %copy-start.2 = (f32[4,5120]{1,0:T(4,128)S(1)}, f32[4,5120]{1,0:T(4,128)}, u32[]{:S(2)}) copy-start(f32[4,5120]{1,0:T(4,128)} %param.12) | copy-start | bytes 245764
  304.2 219.8 %all-gather.3.cloned.1.call-start = ((), (), s32[]{:S(2)}) async-start(), calls=%async_computation.3 | async-start | bytes 9461760 | tf_op jit(solution)/shard_map/all_gather | solution.py:86
  304.8 391.4 %all-gather.5.cloned.1.call-start = ((), (), s32[]{:S(2)}) async-start(), calls=%async_computation.4 | async-start | bytes 9461760 | tf_op jit(solution)/shard_map/all_gather | solution.py:93
  305.4 470.8 %reduce-scatter.2.cloned.1.call-start = ((), (), s32[]{:S(2)}) async-start(), calls=%async_computation.5 | async-start | bytes 4423680 | tf_op jit(solution)/shard_map/reduce_scatter | solution.py:97
  450.5 3.2 copy-start
Sparse Core Ops, SparseCore 0:
  304.3 141.4 all-reduce.1
  718.6 57.5 reduce-scatter.1
Sparse Core Ops, SparseCore 1:
  306.5 217.5 all-gather.2
  525.7 170.5 all-gather.4
where the time goes:
time: 789 us; the launch traced here: 786 us
  waiting for transfers between devices  601 us (76%)
  local copies, waits for them, and re-layouts  62.3 us (8%)
  matrix products  49.6 us (6%)
  starting transfers between devices  36.5 us (5%)
  other arithmetic  21.5 us (3%)
  between operations  15.1 us (2%)
    all_gather x1, waiting for transfers between devices, shards(): lax.all_gather(down_weight, 'frame', axis=1, tiled=True)  172 us
    psum x1, waiting for transfers between devices, shards(): lax.psum(partial_value.astype(jnp.bfloat16), 'head').astype(jnp.float32)  140 us
    ppermute x8, waiting for transfers between devices, shifted(): return lax.ppermute(block, axis, route)  122 us
    all_gather x1, waiting for transfers between devices, shards(): lax.all_gather(up_weight, 'frame', axis=0, tiled=True)  69.3 us
    reduce_scatter x1, waiting for transfers between devices, shards(): lax.psum_scatter(down_terms.astype(jnp.bfloat16), 'head', scatter_dimensi...  57.7 us
    all_to_all x1, waiting for transfers between devices, shards(): lax.all_to_all(qkv, 'head', split_axis=2, concat_axis=0, tiled=True)  38.3 us
    unnamed x21, local copies, waits for them, and re-layouts  34.1 us
    ppermute x8, starting transfers between devices, shifted(): return lax.ppermute(block, axis, route)  28.6 us
  transfers between devices with their start and end apart: 13, of which 11 were waited for; matrix products, arithmetic and copies ran while one was open for 2% of the time, Pallas kernels for 0%

commit v1 on v0

v1 whole, which is shorter than its diff:
```python
import functools
import math

import jax
import jax.numpy as jnp
from jax import lax
from jax.experimental import pallas as pl
from jax.experimental.pallas import tpu as pltpu
from jax.sharding import PartitionSpec as P

HD = 128
SLOTS = 9
BLOCK = 384
NBLK = 32
N_HEAD = 8
ROWS = BLOCK // N_HEAD
GROUP = 5
INNER = GROUP * HD
D = 5120
MESH = pl.DeviceIdType.MESH
MIB = 2**20

partner_offsets = (0, -8, -4, -2, -1, 1, 2, 4, 8)
SLOT = {offset: slot for slot, offset in enumerate(partner_offsets)}
QUERY_ROWS = 128
SCALE_LOG2 = math.log2(math.e) / math.sqrt(HD)


def attention_kernel(
    qkv_ref, band_ref, weight_ref, out_ref,
    heads, attended, weight,
    a2a_send, a2a_recv, own_sem, halo_send, halo_recv, weight_sem,
):
    me = lax.axis_index("head")
    block = lax.axis_index("frame")
    x = lax.rem(block, 4)
    row_start = block - x

    def frame_device(frame):
        return {"head": me, "frame": frame}

    def head_device(head):
        return {"head": head, "frame": block}

    barrier = pltpu.get_barrier_semaphore()
    for k in range(1, N_HEAD):
        pl.semaphore_signal(barrier, inc=1, device_id=head_device(lax.rem(me + k, N_HEAD)), device_id_type=MESH)
    for k in range(1, 4):
        pl.semaphore_signal(barrier, inc=1, device_id=frame_device(row_start + lax.rem(x + k, 4)), device_id_type=MESH)
    for k in (4, NBLK - 4):
        pl.semaphore_signal(barrier, inc=1, device_id=frame_device(lax.rem(block + k, NBLK)), device_id_type=MESH)
    pl.semaphore_wait(barrier, N_HEAD - 1 + 3 + 2)

    fetch_weight = pltpu.make_async_copy(weight_ref, weight, weight_sem)
    my_rows = pl.ds(pl.multiple_of(me * ROWS, 16), ROWS)

    def to_peer(j, k):
        peer = lax.rem(me + k, N_HEAD)
        columns = pl.ds(pl.multiple_of(peer * INNER + j * HD, HD), HD)
        return pltpu.make_async_remote_copy(
            qkv_ref.at[:, :, columns], heads.at[j, :, 0, my_rows],
            a2a_send.at[j, k - 1], a2a_recv.at[j, k - 1],
            device_id=head_device(peer), device_id_type=MESH,
        )

    def own_piece(j):
        columns = pl.ds(pl.multiple_of(me * INNER + j * HD, HD), HD)
        return pltpu.make_async_copy(
            qkv_ref.at[:, :, columns], heads.at[j, :, 0, my_rows], own_sem.at[j]
        )

    def send_heads(j, carry):
        for k in (4, 3, 5, 2, 6, 1, 7):
            to_peer(j, k).start()
        own_piece(j).start()
        return carry

    lax.fori_loop(0, GROUP, send_heads, 0)
    fetch_weight.start()

    low4, high4 = block >= 4, block < NBLK - 4
    routes = (
        (1, 0, -4, block + 4, high4),
        (1, 0, 4, block - 4, low4),
        (1, 0, -1, block + 1, x < 3),
        (1, 0, 1, block - 1, x > 0),
        (2, -4, -8, block + 4, low4 & high4),
        (2, 4, 8, block - 4, low4 & high4),
        (2, -4, -1, row_start, (x == 3) & low4),
        (2, 4, 1, row_start + 3, (x == 0) & high4),
        (2, -1, -2, block + 1, (x == 1) | (x == 2)),
        (2, 1, 2, block - 1, (x == 1) | (x == 2)),
        (2, -4, -2, row_start, (x == 2) & low4),
        (2, 4, 2, row_start + 3, (x == 1) & high4),
        (3, -1, -2, block + 1, (x == 0) & low4),
        (3, 1, 2, block - 1, (x == 3) & high4),
    )
    arrivals = (
        (2, -4, low4),
        (2, 4, high4),
        (2, -1, x > 0),
        (2, 1, x < 3),
        (3, -1, (x == 0) & low4),
        (3, 1, (x == 3) & high4),
        (4, -2, block >= 2),
        (4, 2, block < NBLK - 2),
        (4, -8, block >= 8),
        (4, 8, block < NBLK - 8),
    )

    def route_copy(j, index):
        _, source, target, frame, _ = routes[index]
        return pltpu.make_async_remote_copy(
            heads.at[j, 1:3, SLOT[source]], heads.at[j, 1:3, SLOT[target]],
            halo_send.at[j, index], halo_recv.at[j, SLOT[target] - 1],
            device_id=frame_device(jnp.clip(frame, 0, NBLK - 1)), device_id_type=MESH,
        )

    def send_stage(j, stage):
        for index, route in enumerate(routes):
            if route[0] == stage:
                @pl.when(route[4])
                def _():
                    route_copy(j, index).start()

    def wait_stage(j, stage):
        for before, slot, when in arrivals:
            if before == stage:
                @pl.when(when)
                def _():
                    landed = heads.at[j, 1:3, SLOT[slot]]
                    pltpu.make_async_copy(landed, landed, halo_recv.at[j, SLOT[slot] - 1]).wait()

    for offset in partner_offsets[1:]:
        partner = block + offset

        @pl.when((partner < 0) | (partner >= NBLK))
        def _():
            heads[:, 1:3, SLOT[offset]] = jnp.zeros((GROUP, 2, BLOCK, HD), jnp.bfloat16)

    def attend(j):
        widths = []
        for slot, offset in enumerate(partner_offsets):
            partner = block + offset
            present = (partner >= 0) & (partner < NBLK)
            widths.append(jnp.where(present, band_ref[0, slot], 0))
        keys = heads[j, 1].reshape(SLOTS * BLOCK, HD)
        values = heads[j, 2].reshape(SLOTS * BLOCK, HD)
        columns = pl.ds(pl.multiple_of(j * HD, HD), HD)
        for first in range(0, BLOCK, QUERY_ROWS):
            queries = heads[j, 0, 0, first:first + QUERY_ROWS]
            scores = lax.dot_general(
                queries, keys, (((1,), (1,)), ((), ())), preferred_element_type=jnp.float32
            )
            row = lax.broadcasted_iota(jnp.int32, (QUERY_ROWS, BLOCK), 0) + first
            column = lax.broadcasted_iota(jnp.int32, (QUERY_ROWS, BLOCK), 1)
            distance = jnp.abs(row - column)
            parts = []
            for slot in range(SLOTS):
                part = scores[:, slot * BLOCK:(slot + 1) * BLOCK]
                parts.append(jnp.where(distance < widths[slot], part, -1e30))
            top = functools.reduce(jnp.maximum, parts)
            row_max = jnp.max(top, axis=1, keepdims=True)
            weights = [jnp.exp2((part - row_max) * SCALE_LOG2) for part in parts]
            denominator = jnp.sum(functools.reduce(jnp.add, weights), axis=1, keepdims=True)
            probabilities = jnp.concatenate([w.astype(jnp.bfloat16) for w in weights], axis=1)
            summed = jnp.dot(probabilities, values, preferred_element_type=jnp.float32)
            attended[first:first + QUERY_ROWS, columns] = (summed / denominator).astype(jnp.bfloat16)

    def step(it, carry):
        @pl.when(it < GROUP)
        def _():
            for k in range(1, N_HEAD):
                origin = lax.rem(me + N_HEAD - k, N_HEAD)
                landed = heads.at[it, :, 0, pl.ds(pl.multiple_of(origin * ROWS, 16), ROWS)]
                pltpu.make_async_copy(landed, landed, a2a_recv.at[it, k - 1]).wait()
            own_piece(it).wait()
            send_stage(it, 1)

        @pl.when((it >= 1) & (it < GROUP + 1))
        def _():
            wait_stage(it - 1, 2)
            send_stage(it - 1, 2)

        @pl.when((it >= 2) & (it < GROUP + 2))
        def _():
            wait_stage(it - 2, 3)
            send_stage(it - 2, 3)

        @pl.when(it >= 3)
        def _():
            wait_stage(it - 3, 4)
            attend(it - 3)

        return carry

    lax.fori_loop(0, GROUP + 3, step, 0)

    fetch_weight.wait()

    def project(c, carry):
        columns = pl.ds(pl.multiple_of(c * 512, 512), 512)
        out_ref[:, columns] = jnp.dot(
            attended[...], weight[:, columns], preferred_element_type=jnp.float32
        ).astype(jnp.bfloat16)
        return carry

    lax.fori_loop(0, D // 512, project, 0)

    def finish(j, carry):
        for k in range(1, N_HEAD):
            to_peer(j, k).wait_send()
        for index, route in enumerate(routes):
            @pl.when(route[4])
            def _():
                route_copy(j, index).wait_send()
        return carry

    lax.fori_loop(0, GROUP, finish, 0)


def attention(qkv, band, out_weight):
    return pl.pallas_call(
        attention_kernel,
        out_shape=jax.ShapeDtypeStruct((BLOCK, D), jnp.bfloat16),
        in_specs=[
            pl.BlockSpec(memory_space=pl.ANY),
            pl.BlockSpec(memory_space=pltpu.SMEM),
            pl.BlockSpec(memory_space=pl.ANY),
        ],
        out_specs=pl.BlockSpec(memory_space=pltpu.VMEM),
        scratch_shapes=[
            pltpu.VMEM((GROUP, 3, SLOTS, BLOCK, HD), jnp.bfloat16),
            pltpu.VMEM((BLOCK, INNER), jnp.bfloat16),
            pltpu.VMEM((INNER, D), jnp.bfloat16),
            pltpu.SemaphoreType.DMA((GROUP, N_HEAD - 1)),
            pltpu.SemaphoreType.DMA((GROUP, N_HEAD - 1)),
            pltpu.SemaphoreType.DMA((GROUP,)),
            pltpu.SemaphoreType.DMA((GROUP, 14)),
            pltpu.SemaphoreType.DMA((GROUP, SLOTS - 1)),
            pltpu.SemaphoreType.DMA,
        ],
        compiler_params=pltpu.CompilerParams(
            collective_id=0, has_side_effects=True, vmem_limit_bytes=56 * MIB
        ),
        name="attention",
    )(qkv, band, out_weight)


def rounded(values):
    narrow = lax.optimization_barrier(values.astype(jnp.bfloat16))
    return narrow.astype(jnp.float32)


def modulate(residual_state, shift_row, scale_row):
    average = jnp.mean(residual_state, axis=-1, keepdims=True)
    centered = residual_state - average
    variance = jnp.mean(centered * centered, axis=-1, keepdims=True)
    normal_form = centered * lax.rsqrt(variance + 1e-06)
    return (normal_form * (1.0 + scale_row) + shift_row).astype(jnp.bfloat16)


def shards(resid, qkv, band, out_weight, modulation, up_weight, down_weight):
    head_count = lax.axis_size("head")
    head_index = lax.axis_index("head")
    partial_value = attention(jnp.transpose(qkv, (1, 0, 2)), band, out_weight)
    rows_dev = BLOCK // head_count
    first_row = head_index * rows_dev
    branch = lax.psum(partial_value, "head").astype(jnp.float32)
    residual_state = resid.astype(jnp.float32) + modulation[0] * branch
    normed = modulate(residual_state, modulation[1], modulation[2])
    state_rows = lax.dynamic_slice_in_dim(residual_state, first_row, rows_dev, 0)
    projected = jnp.dot(
        normed,
        lax.all_gather(up_weight, "frame", axis=0, tiled=True),
        preferred_element_type=jnp.float32,
    )
    hidden = jax.nn.gelu(projected, approximate=True).astype(jnp.bfloat16)
    down_terms = rounded(
        jnp.dot(
            hidden,
            lax.all_gather(down_weight, "frame", axis=1, tiled=True),
            preferred_element_type=jnp.float32,
        )
    )
    ffn_out = lax.psum_scatter(
        down_terms.astype(jnp.bfloat16), "head", scatter_dimension=0, tiled=True
    ).astype(jnp.float32)
    return (state_rows + modulation[3] * ffn_out).astype(jnp.bfloat16)


def solution(mesh):
    in_specs = (
        P("frame", None),
        P(("frame", "head"), None, None),
        P("frame", None),
        P("head", None),
        P(),
        P("frame", "head"),
        P("head", "frame"),
    )
    out_specs = P(("frame", "head"), None)
    return jax.shard_map(shards, mesh=mesh, in_specs=in_specs, out_specs=out_specs, check_vma=False)
```

time: 789 us -> 607 us (0.77)
  waiting for transfers between devices: 601 us -> 440 us
  Pallas kernels: 0 us -> 117 us
  local copies, waits for them, and re-layouts: 62.3 us -> 3.14 us
  starting transfers between devices: 36.5 us -> 0.31 us
  matrix products: 49.6 us -> 22.3 us
  other arithmetic: 21.5 us -> 8.01 us
    ppermute x8 -> x0, waiting for transfers between devices: 122 us -> none  [shifted(): return lax.ppermute(block, axis, route)]
    pallas_call x0 -> x1, Pallas kernels: none -> 117 us  [attention(): pl.pallas_call(attention_kernel, out_shape=jax.ShapeDtypeStruct((BLOCK, D...]
    all_to_all x1 -> x0, waiting for transfers between devices: 38.3 us -> none  [shards(): lax.all_to_all(qkv, 'head', split_axis=2, concat_axis=0, tiled=True)]
    unnamed x21 -> x4, local copies, waits for them, and re-layouts: 34.1 us -> 3.14 us
    ppermute x8 -> x0, starting transfers between devices: 28.6 us -> none  [shifted(): return lax.ppermute(block, axis, route)]
    dot_general x3 -> x0, matrix products: 27.3 us -> none  [the longest x1 14.2 us: shards(): jnp.einsum('igd,sjgd->gisj', queries, key_rows, preferred_element_type=jn...]
    slice x6 -> x0, local copies, waits for them, and re-layouts: 22.2 us -> none  [the longest x2 12.1 us: shards(): key_rows = stacked[:, :, 0].reshape(SLOTS, block_len, head_group, HD)]
    reduce_sum x1 -> x0, other arithmetic: 12.5 us -> none  [shards(): denominator = jnp.sum(weights, axis=(2, 3))]
  transfers between devices with their start and end apart: 13 -> 4, of which waited for: 11 -> 4; matrix products, arithmetic and copies ran while one was open for 2% -> 1% of each run, Pallas kernels for 0% -> 0%
where the time goes in v1:
time: 607 us; the launch traced here: 606 us
  waiting for transfers between devices  440 us (72%)
  Pallas kernels  117 us (19%)
  matrix products  22.3 us (4%)
  between operations  14.9 us (2%)
  other arithmetic  8.01 us (1%)
    all_gather x1, waiting for transfers between devices, shards(): lax.all_gather(down_weight, 'frame', axis=1, tiled=True)  173 us
    psum x1, waiting for transfers between devices, shards(): branch = lax.psum(partial_value, 'head').astype(jnp.float32)  140 us
    pallas_call x1, Pallas kernels, attention(): pl.pallas_call(attention_kernel, out_shape=jax.ShapeDtypeStruct((BLOCK, D...  117 us
    all_gather x1, waiting for transfers between devices, shards(): lax.all_gather(up_weight, 'frame', axis=0, tiled=True)  68.7 us
    reduce_scatter x1, waiting for transfers between devices, shards(): lax.psum_scatter(down_terms.astype(jnp.bfloat16), 'head', scatter_dimensi...  57.8 us
    dot_general x1, matrix products, shards(): jnp.dot(hidden, lax.all_gather(down_weight, 'frame', axis=1, tiled=True),...  22.3 us
  transfers between devices with their start and end apart: 4, of which 4 were waited for; matrix products, arithmetic and copies ran while one was open for 1% of the time, Pallas kernels for 0%

profile of v1, /device:TPU:32, one launch (start us, length us, event | category | flops | bytes accessed | tf_op | source)
XLA Modules:
  0.0 605.8 jit_solution(6480027916628807981)
XLA Ops:
  7.4 0.0 all-reduce.2.cloned.1.call-start
  7.4 0.0 copy-start.1
  7.4 117.3 %attention.1 = bf16[384,5120]{1,0:T(8,128)(2,1)} custom-call(bf16[3,48,5120]{2,1,0:T(8,128)(2,1)} %bitcast.7, s32[1,9]{1,0:T(1,128)} %band_ref.1, bf16[640,5120]{1,0:T(8,128)(2,1)} %weight_ref.1), custom_call_target="tpu_custom_call" | custom-call | tf_op jit(solution)/shard_map/attention/pallas_call | solution.py:223
  124.7 0.0 all-reduce.2.cloned.1.call-update
  124.7 0.0 all-gather.3.cloned.1.call-start
  124.8 0.5 all-gather.3.cloned.1.call-update
  125.3 0.0 all-gather.5.cloned.1.call-start
  125.4 0.5 all-gather.5.cloned.1.call-update
  125.9 0.2 reduce-scatter.2.cloned.1.call-start
  126.1 0.0 copy-done.1
  126.2 0.1 fusion.18
  126.2 139.6 %all-reduce.2.cloned.1.call-done = bf16[384,5120]{1,0:T(8,128)(2,1)} async-done(((bf16[384,5120]{1,0:T(8,128)(2,1)}), bf16[384,5120]{1,0:T(8,128)(2,1)}) %all-reduce.2.cloned.1.call-update) | async-done | bytes 3932176 | tf_op jit(solution)/shard_map/psum | solution.py:269
  265.9 4.8 fusion.17
  270.6 0.0 copy-start
  270.7 3.1 copy-done
  273.8 0.9 multiply_reduce_fusion
  274.7 68.7 %all-gather.3.cloned.1.call-done = bf16[5120,864]{1,0:T(8,128)(2,1)} async-done(((bf16[160,864]{1,0:T(8,128)(2,1)}), bf16[5120,864]{1,0:T(8,128)(2,1)}) %all-gather.3.cloned.1.call-update) | async-done | bytes 8847376 | tf_op jit(solution)/shard_map/all_gather | solution.py:275
  343.4 172.5 %all-gather.5.cloned.1.call-done = bf16[864,5120]{0,1:T(8,128)(2,1)} async-done(((bf16[864,160]{0,1:T(8,128)(2,1)}), bf16[864,5120]{0,1:T(8,128)(2,1)}) %all-gather.5.cloned.1.call-update) | async-done | bytes 8847376 | tf_op jit(solution)/shard_map/all_gather | solution.py:282
  516.0 22.3 %convolution_convert_fusion = bf16[384,5120]{1,0:T(8,128)(2,1)} fusion(bf16[864,5120]{0,1:T(8,128)(2,1)} %all-gather.5.cloned.1.call-done, bf16[5120,864]{1,0:T(8,128)(2,1)} %all-gather.3.cloned.1.call-done, f32[384,5120]{1,0:T(8,128)} %copy-done, f32[5120]{0:T(1024)S(1)} %bitcast.10, f32[5120]{0:T(1024)S(1)} %bitcast.11, f32[384]{0:T(512)S(1)} %add_rsqrt_fusion, ...), kind=kOutput, calls=%fused_computation.3 | convolution fusion | flops 6809554944 | bytes 29535232 | tf_op jit(solution)/shard_map/dot_general | solution.py:280
  538.3 0.0 reduce-scatter.2.cloned.1.call-update
  538.3 57.8 %reduce-scatter.2.cloned.1.call-done = bf16[48,5120]{1,0:T(8,128)(2,1)} async-done(((bf16[384,5120]{1,0:T(8,128)(2,1)}), bf16[48,5120]{1,0:T(8,128)(2,1)}) %reduce-scatter.2.cloned.1.call-update) | async-done | bytes 491536 | tf_op jit(solution)/shard_map/reduce_scatter | solution.py:286
  596.1 2.2 add_convert_fusion.4
  (2 shorter events, 0.0 us)
Async XLA Ops:
  7.4 258.5 %all-reduce.2.cloned.1.call-start = ((), (), s32[]{:S(2)}) async-start(), calls=%async_computation.1 | async-start | bytes 7864320 | tf_op jit(solution)/shard_map/psum | solution.py:269
  7.4 118.8 %copy-start.1 = (f32[4,5120]{1,0:T(4,128)S(1)}, f32[4,5120]{1,0:T(4,128)}, u32[]{:S(2)}) copy-start(f32[4,5120]{1,0:T(4,128)} %param.11) | copy-start | bytes 245764
  124.7 218.7 %all-gather.3.cloned.1.call-start = ((), (), s32[]{:S(2)}) async-start(), calls=%async_computation.2 | async-start | bytes 9461760 | tf_op jit(solution)/shard_map/all_gather | solution.py:275
  125.3 390.6 %all-gather.5.cloned.1.call-start = ((), (), s32[]{:S(2)}) async-start(), calls=%async_computation.3 | async-start | bytes 9461760 | tf_op jit(solution)/shard_map/all_gather | solution.py:282
  125.9 470.2 %reduce-scatter.2.cloned.1.call-start = ((), (), s32[]{:S(2)}) async-start(), calls=%async_computation.4 | async-start | bytes 4423680 | tf_op jit(solution)/shard_map/reduce_scatter | solution.py:286
  270.6 3.2 copy-start
Sparse Core Ops, SparseCore 0:
  124.9 140.9 all-reduce.1
  538.5 57.6 reduce-scatter.1
Sparse Core Ops, SparseCore 1:
  127.0 216.4 all-gather.2
  345.1 170.8 all-gather.4

commit v2 on v1

--- a/solution.py
+++ b/solution.py
@@ -247,46 +247,364 @@
     )(qkv, band, out_weight)
 
 
-def rounded(values):
-    narrow = lax.optimization_barrier(values.astype(jnp.bfloat16))
-    return narrow.astype(jnp.float32)
-
-
-def modulate(residual_state, shift_row, scale_row):
-    average = jnp.mean(residual_state, axis=-1, keepdims=True)
-    centered = residual_state - average
-    variance = jnp.mean(centered * centered, axis=-1, keepdims=True)
-    normal_form = centered * lax.rsqrt(variance + 1e-06)
-    return (normal_form * (1.0 + scale_row) + shift_row).astype(jnp.bfloat16)
+HALF = D // 2
+UNITS = 432
+MAIN = 384
+TAIL = UNITS - MAIN
+PACK = 896
+WROWS = 160
+
+
+def feed_forward_kernel(
+    partial_ref, resid_ref, modulation_ref, pack_own_ref, pack_other_ref, out_ref,
+    weights, sib1, opposite, pairs, state, resid_rows, normed, hidden, down, sib2, ring,
+    local_sem, w_send, w_recv, s1_send, s1_recv, r1_send, r1_recv,
+    ag_send, ag_recv, agsib_send, agsib_recv, s2_send, s2_recv, r2_send, r2_recv,
+):
+    me = lax.axis_index("head")
+    frame = lax.axis_index("frame")
+    z_hi, core = me // 2, lax.rem(me, 2)
+    z_lo, yx = frame // 16, lax.rem(frame, 16)
+    y, x = yx // 4, lax.rem(yx, 4)
+    z = z_hi * 2 + z_lo
+    halves = (pl.ds(0, HALF), pl.ds(HALF, HALF))
+
+    def z_device(other):
+        return {"head": (other // 2) * 2 + core, "frame": lax.rem(other, 2) * 16 + yx}
+
+    sibling = {"head": z_hi * 2 + 1 - core, "frame": frame}
+    above, below = z_device(lax.rem(z + 1, 8)), z_device(lax.rem(z + 7, 8))
+    above2, below2 = z_device(lax.rem(z + 2, 8)), z_device(lax.rem(z + 6, 8))
+    x_peers = [{"head": me, "frame": z_lo * 16 + y * 4 + lax.rem(x + k, 4)} for k in (1, 2, 3)]
+    y_peers = [{"head": me, "frame": z_lo * 16 + lax.rem(y + k, 4) * 4 + x} for k in (1, 2, 3)]
+    other_plane = z_device(z + 1 - 2 * z_lo)
+
+    barrier = pltpu.get_barrier_semaphore()
+    greeted = [sibling, above, below, above2, below2] + x_peers + y_peers
+    for device in greeted:
+        pl.semaphore_signal(barrier, inc=1, device_id=device, device_id_type=MESH)
+    pl.semaphore_wait(barrier, len(greeted))
+
+    def remote(source, target, send, recv, device):
+        return pltpu.make_async_remote_copy(
+            source, target, send, recv, device_id=device, device_id_type=MESH
+        )
+
+    started = []
+
+    def go(copy):
+        copy.start()
+        started.append(copy)
+
+    my_rows = pl.ds(pl.multiple_of(me * ROWS, 16), ROWS)
+    fetch_resid = pltpu.make_async_copy(resid_ref.at[my_rows], resid_rows, local_sem.at[0])
+    fetch_resid.start()
+    fetch_pack = pltpu.make_async_copy(pack_own_ref, weights.at[z_lo, y, x], local_sem.at[1])
+    fetch_pack.start()
+
+    order = [lax.rem(z_hi + k, 4) for k in (2, 1, 3, 0)]
+    s1 = [
+        remote(partial_ref.at[q, 1 - core], sib1.at[q], s1_send.at[i], s1_recv.at[i], sibling)
+        for i, q in enumerate(order)
+    ]
+    for copy in s1:
+        go(copy)
+
+    cross = remote(pack_other_ref, weights.at[z_lo, y, x], w_send.at[0], w_recv.at[0], other_plane)
+    go(cross)
+    first_a = [
+        remote(pack_own_ref, weights.at[z_lo, y, x], w_send.at[1 + i], w_recv.at[1 + i], device)
+        for i, device in enumerate(x_peers)
+    ]
+    for copy in first_a:
+        go(copy)
+
+    def pair(q, columns):
+        return (
+            partial_ref[q, core, :, columns].astype(jnp.float32)
+            + sib1[q, :, columns].astype(jnp.float32)
+        )
+
+    s1[0].wait_recv()
+    q = order[0]
+    for half in (0, 1):
+        sib1[q, :, halves[half]] = pair(q, halves[half]).astype(jnp.bfloat16)
+        go(remote(
+            sib1.at[q, :, halves[half]], opposite.at[half],
+            r1_send.at[half], r1_recv.at[half], (above2, below2)[half],
+        ))
+    opposites = started[-2:]
+    finals = [None] * 4
+    for way in (0, 1):
+        s1[1 + way].wait_recv()
+        q, half = order[1 + way], 1 - way
+        sib1[q, :, halves[half]] = pair(q, halves[half]).astype(jnp.bfloat16)
+        index = 2 + way * 2 + half
+        go(remote(
+            sib1.at[q, :, halves[half]], pairs.at[way, :, halves[half]],
+            r1_send.at[index], r1_recv.at[index], (above2, below2)[way],
+        ))
+        finals[way * 2 + half] = started[-1]
+
+    cross.wait_recv()
+    first_b = [
+        remote(
+            weights.at[1 - z_lo, y, x], weights.at[1 - z_lo, y, x],
+            w_send.at[4 + i], w_recv.at[4 + i], device,
+        )
+        for i, device in enumerate(y_peers)
+    ]
+    for copy in first_b:
+        go(copy)
+
+    for way in (0, 1):
+        q, half = order[1 + way], way
+        opposites[half].wait_recv()
+        total = pair(q, halves[half]) + opposite[half].astype(jnp.float32)
+        sib1[q, :, halves[half]] = total.astype(jnp.bfloat16)
+        index = 2 + way * 2 + half
+        go(remote(
+            sib1.at[q, :, halves[half]], pairs.at[way, :, halves[half]],
+            r1_send.at[index], r1_recv.at[index], (above2, below2)[way],
+        ))
+        finals[way * 2 + half] = started[-1]
+
+    fetch_pack.wait()
+    for copy in first_a:
+        copy.wait_recv()
+    second_a = [
+        remote(
+            weights.at[z_lo, y], weights.at[z_lo, y], w_send.at[7 + i], w_recv.at[7 + i], device
+        )
+        for i, device in enumerate(y_peers)
+    ]
+    for copy in second_a:
+        go(copy)
+    for copy in first_b:
+        copy.wait_recv()
+    second_b = [
+        remote(
+            weights.at[1 - z_lo, :, x], weights.at[1 - z_lo, :, x],
+            w_send.at[10 + i], w_recv.at[10 + i], device,
+        )
+        for i, device in enumerate(x_peers)
+    ]
+    for copy in second_b:
+        go(copy)
+
+    fetch_resid.wait()
+    s1[3].wait_recv()
+    for copy in finals:
+        copy.wait_recv()
+    for half in (0, 1):
+        columns = halves[half]
+        branch = (
+            pair(z_hi, columns)
+            + pairs[0, :, columns].astype(jnp.float32)
+            + pairs[1, :, columns].astype(jnp.float32)
+        )
+        state[:, columns] = (
+            resid_rows[:, columns].astype(jnp.float32) + modulation_ref[0:1, columns] * branch
+        )
+    for first in range(0, ROWS, 16):
+        rows = slice(first, first + 16)
+        value = state[rows]
+        average = jnp.mean(value, axis=-1, keepdims=True)
+        centered = value - average
+        variance = jnp.mean(centered * centered, axis=-1, keepdims=True)
+        normal_form = centered * lax.rsqrt(variance + 1e-06)
+        normed[z, core, rows] = (
+            normal_form * (1.0 + modulation_ref[2:3]) + modulation_ref[1:2]
+        ).astype(jnp.bfloat16)
+
+    def shard(distance):
+        return lax.rem(z + distance + 8, 8)
+
+    gathered = []
+
+    def to_sibling(view, index):
+        copy = remote(view, view, agsib_send.at[index], agsib_recv.at[index], sibling)
+        go(copy)
+        gathered.append(copy)
+
+    hops = {}
+
+    def hop(way, step):
+        origin = shard((1 - step) * (1 - 2 * way))
+        view = normed.at[origin, core]
+        if step == 4:
+            view = view.at[:, halves[way]]
+        hops[way, step] = remote(
+            view, view, ag_send.at[way, step - 1], ag_recv.at[way, step - 1], (above, below)[way]
+        )
+        go(hops[way, step])
+
+    hop(0, 1)
+    hop(1, 1)
+    to_sibling(normed.at[z, core], 0)
+    for step in (1, 2, 3, 4):
+        for way in (0, 1):
+            hops[way, step].wait_recv()
+            view = normed.at[shard(-step * (1 - 2 * way)), core]
+            if step < 4:
+                hop(way, step + 1)
+            else:
+                view = view.at[:, halves[way]]
+            to_sibling(view, 1 + (step - 1) * 2 + way)
+    for copy in gathered:
+        copy.wait_recv()
+    for copy in second_a + second_b:
+        copy.wait_recv()
+
+    def up(i, carry):
+        rows = normed[pl.ds(4 * i, 4)].reshape(4 * 2 * ROWS, D)
+        total = None
+        for c in range(4):
+            weight = weights[c // 2, 2 * (c % 2):2 * (c % 2) + 2, :, :, 0:512].reshape(8 * WROWS, 512)
+            product = jnp.dot(
+                rows[:, c * 1280:(c + 1) * 1280], weight, preferred_element_type=jnp.float32
+            )
+            total = product if total is None else total + product
+        active = jax.nn.gelu(total, approximate=True)
+        lane = lax.broadcasted_iota(jnp.int32, (8 * ROWS, 128), 1)
+        tail = pltpu.roll(active[:, MAIN:512], TAIL, 1)
+        tail = jnp.where((lane >= TAIL) & (lane < 2 * TAIL), tail, 0.0)
+        target = pl.ds(pl.multiple_of(i * 8 * ROWS, 16), 8 * ROWS)
+        hidden[target, 0:128] = tail.astype(jnp.bfloat16)
+        hidden[target, 128:512] = active[:, 0:MAIN].astype(jnp.bfloat16)
+        return carry
+
+    lax.fori_loop(0, 2, up, 0)
+
+    def project(c, carry):
+        weight = weights[c // 4, lax.rem(c, 4), :, :, MAIN:PACK].reshape(4 * WROWS, 512)
+        columns = pl.ds(pl.multiple_of(c * 4 * WROWS, 128), 4 * WROWS)
+        product = lax.dot_general(
+            hidden[...], weight, (((1,), (1,)), ((), ())), preferred_element_type=jnp.float32
+        )
+        down[:, :, :, columns] = product.astype(jnp.bfloat16).reshape(8, 2, ROWS, 4 * WROWS)
+        return carry
+
+    s2 = {}
+    distances = (4, 3, -3, 2, -2, 1, -1, 0)
+    for half in (0, 1):
+        lax.fori_loop(4 * half, 4 * half + 4, project, 0)
+        for i, distance in enumerate(distances):
+            q = shard(distance)
+            s2[distance, half] = remote(
+                down.at[q, 1 - core, :, halves[half]], sib2.at[q, :, halves[half]],
+                s2_send.at[half, i], s2_recv.at[half, i], sibling,
+            )
+            go(s2[distance, half])
+
+    def pair2(q, columns):
+        return (
+            down[q, core, :, columns].astype(jnp.float32)
+            + sib2[q, :, columns].astype(jnp.float32)
+        )
+
+    sums = {}
+
+    def ring_step(way, half, step):
+        distance = (5 - step) * (1 - 2 * way)
+        key = 4 if step == 1 else distance
+        q, columns = shard(distance), halves[half]
+        s2[key, half].wait_recv()
+        total = pair2(q, columns)
+        if (way, half, step - 1) in sums:
+            sums[way, half, step - 1].wait_recv()
+            total = total + ring[way, half, step - 2].astype(jnp.float32)
+        sib2[q, :, columns] = total.astype(jnp.bfloat16)
+        sums[way, half, step] = remote(
+            sib2.at[q, :, columns], ring.at[way, half, step - 1],
+            r2_send.at[way, half, step - 1], r2_recv.at[way, half, step - 1],
+            (above, below)[way],
+        )
+        go(sums[way, half, step])
+
+    ring_step(0, 0, 1)
+    ring_step(1, 1, 1)
+    for step in (2, 3, 4):
+        ring_step(0, 1, step)
+        ring_step(1, 0, step)
+        ring_step(0, 0, step)
+        ring_step(1, 1, step)
+    for half in (1, 0):
+        columns = halves[half]
+        s2[0, half].wait_recv()
+        ffn = pair2(z, columns)
+        for way in ((0, 1) if half else (1, 0)):
+            sums[way, half, 4].wait_recv()
+            ffn = ffn + ring[way, half, 3].astype(jnp.float32)
+        out_ref[:, columns] = (
+            state[:, columns] + modulation_ref[3:4, columns] * ffn
+        ).astype(jnp.bfloat16)
+
+    for copy in started:
+        copy.wait_send()
+
+
+def feed_forward(partial_value, resid, modulation, pack_own, pack_other):
+    dma = pltpu.SemaphoreType.DMA
+    bf16 = jnp.bfloat16
+    return pl.pallas_call(
+        feed_forward_kernel,
+        out_shape=jax.ShapeDtypeStruct((ROWS, D), bf16),
+        in_specs=[
+            pl.BlockSpec(memory_space=pltpu.VMEM),
+            pl.BlockSpec(memory_space=pl.ANY),
+            pl.BlockSpec(memory_space=pltpu.VMEM),
+            pl.BlockSpec(memory_space=pl.ANY),
+            pl.BlockSpec(memory_space=pl.ANY),
+        ],
+        out_specs=pl.BlockSpec(memory_space=pltpu.VMEM),
+        scratch_shapes=[
+            pltpu.VMEM((2, 4, 4, WROWS, PACK), bf16),
+            pltpu.VMEM((4, ROWS, D), bf16),
+            pltpu.VMEM((2, ROWS, HALF), bf16),
+            pltpu.VMEM((2, ROWS, D), bf16),
+            pltpu.VMEM((ROWS, D), jnp.float32),
+            pltpu.VMEM((ROWS, D), bf16),
+            pltpu.VMEM((8, 2, ROWS, D), bf16),
+            pltpu.VMEM((16 * ROWS, 512), bf16),
+            pltpu.VMEM((8, 2, ROWS, D), bf16),
+            pltpu.VMEM((8, ROWS, D), bf16),
+            pltpu.VMEM((2, 2, 4, ROWS, HALF), bf16),
+            dma((2,)), dma((13,)), dma((13,)), dma((4,)), dma((4,)), dma((6,)), dma((6,)),
+            dma((2, 4)), dma((2, 4)), dma((9,)), dma((9,)),
+            dma((2, 8)), dma((2, 8)), dma((2, 2, 4)), dma((2, 2, 4)),
+        ],
+        compiler_params=pltpu.CompilerParams(
+            collective_id=1, has_side_effects=True, vmem_limit_bytes=58 * MIB
+        ),
+        name="feed_forward",
+    )(partial_value, resid, modulation, pack_own, pack_other)
+
+
+def pack_weights(up_weight, down_rows, first):
+    cut = first + MAIN
+    return jnp.concatenate(
+        [
+            up_weight[:, first:cut],
+            up_weight[:, cut:first + UNITS],
+            down_rows[:, cut:first + UNITS],
+            jnp.zeros((WROWS, PACK - MAIN - 2 * TAIL - MAIN), jnp.bfloat16),
+            down_rows[:, first:cut],
+        ],
+        axis=1,
+    )
 
 
 def shards(resid, qkv, band, out_weight, modulation, up_weight, down_weight):
-    head_count = lax.axis_size("head")
-    head_index = lax.axis_index("head")
+    z_lo = lax.axis_index("frame") // 16
+    down_rows = jnp.transpose(down_weight)
+    packs = [pack_weights(up_weight, down_rows, first) for first in (0, UNITS)]
+    pack_own = jnp.where(z_lo == 0, packs[0], packs[1])
+    pack_other = jnp.where(z_lo == 0, packs[1], packs[0])
     partial_value = attention(jnp.transpose(qkv, (1, 0, 2)), band, out_weight)
-    rows_dev = BLOCK // head_count
-    first_row = head_index * rows_dev
-    branch = lax.psum(partial_value, "head").astype(jnp.float32)
-    residual_state = resid.astype(jnp.float32) + modulation[0] * branch
-    normed = modulate(residual_state, modulation[1], modulation[2])
-    state_rows = lax.dynamic_slice_in_dim(residual_state, first_row, rows_dev, 0)
-    projected = jnp.dot(
-        normed,
-        lax.all_gather(up_weight, "frame", axis=0, tiled=True),
-        preferred_element_type=jnp.float32,
+    return feed_forward(
+        partial_value.reshape(4, 2, ROWS, D), resid, modulation, pack_own, pack_other
     )
-    hidden = jax.nn.gelu(projected, approximate=True).astype(jnp.bfloat16)
-    down_terms = rounded(
-        jnp.dot(
-            hidden,
-            lax.all_gather(down_weight, "frame", axis=1, tiled=True),
-            preferred_element_type=jnp.float32,
-        )
-    )
-    ffn_out = lax.psum_scatter(
-        down_terms.astype(jnp.bfloat16), "head", scatter_dimension=0, tiled=True
-    ).astype(jnp.float32)
-    return (state_rows + modulation[3] * ffn_out).astype(jnp.bfloat16)
 
 
 def solution(mesh):

time: 607 us -> 282 us (0.46)
  the two profiles are of different devices: /device:TPU:32 before, /device:TPU:57 now
where the time goes in v2:
time: 282 us; the launch traced here: 281 us
  Pallas kernels  275 us (98%)
  local copies, waits for them, and re-layouts  4.99 us (2%)
    pallas_call x1, Pallas kernels, feed_forward(): pl.pallas_call(feed_forward_kernel, out_shape=jax.ShapeDtypeStruct((ROWS,...  179 us
    pallas_call x1, Pallas kernels, attention(): pl.pallas_call(attention_kernel, out_shape=jax.ShapeDtypeStruct((BLOCK, D...  96.8 us

profile of v2, /device:TPU:57, one launch (start us, length us, event | category | flops | bytes accessed | tf_op | source)
XLA Modules:
  0.0 281.5 jit_solution(5581696239832901665)
XLA Ops:
  0.0 0.1 pad.6.clone
  0.1 0.9 fusion.1
  1.0 1.1 fusion.2
  2.0 1.1 fusion
  3.2 1.0 broadcast_select_fusion
  4.2 96.8 %attention.1 = bf16[384,5120]{1,0:T(8,128)(2,1)} custom-call(bf16[3,48,5120]{2,1,0:T(8,128)(2,1)} %bitcast.4, s32[1,9]{1,0:T(1,128)} %band_ref.1, bf16[640,5120]{1,0:T(8,128)(2,1)} %weight_ref.1), custom_call_target="tpu_custom_call" | custom-call | tf_op jit(solution)/shard_map/attention/pallas_call | solution.py:223
  101.0 178.6 %feed_forward.1 = bf16[48,5120]{1,0:T(8,128)(2,1)} custom-call(bf16[4,2,48,5120]{3,2,1,0:T(8,128)(2,1)} %bitcast.3, bf16[384,5120]{1,0:T(8,128)(2,1)} %resid_ref.1, f32[4,5120]{1,0:T(4,128)} %modulation_ref.1, bf16[160,896]{1,0:T(8,128)(2,1)} %get-tuple-element.6.pack_own_ref, bf16[160,896]{1,0:T(8,128)(2,1)} %get-tuple-element.5.pack_other_ref), custom_call_target="tpu_custom_call" | custom-call | tf_op jit(solution)/shard_map/feed_forward/pallas_call | solution.py:550
  279.6 1.8 copy.9
  (1 shorter events, 0.0 us)

commit v3 on v1

--- a/solution.py
+++ b/solution.py
@@ -75,7 +75,7 @@
         own_piece(j).start()
         return carry
 
-    lax.fori_loop(0, GROUP, send_heads, 0)
+    lax.fori_loop(0, 2, send_heads, 0)
     fetch_weight.start()
 
     low4, high4 = block >= 4, block < NBLK - 4
@@ -177,6 +177,10 @@
             own_piece(it).wait()
             send_stage(it, 1)
 
+        @pl.when(it < GROUP - 2)
+        def _():
+            send_heads(it + 2, 0)
+
         @pl.when((it >= 1) & (it < GROUP + 1))
         def _():
             wait_stage(it - 1, 2)
@@ -247,46 +251,355 @@
     )(qkv, band, out_weight)
 
 
-def rounded(values):
-    narrow = lax.optimization_barrier(values.astype(jnp.bfloat16))
-    return narrow.astype(jnp.float32)
-
-
-def modulate(residual_state, shift_row, scale_row):
-    average = jnp.mean(residual_state, axis=-1, keepdims=True)
-    centered = residual_state - average
-    variance = jnp.mean(centered * centered, axis=-1, keepdims=True)
-    normal_form = centered * lax.rsqrt(variance + 1e-06)
-    return (normal_form * (1.0 + scale_row) + shift_row).astype(jnp.bfloat16)
+HALF = D // 2
+UNITS = 432
+MAIN = 384
+TAIL = UNITS - MAIN
+PACK = 896
+WROWS = 160
+STREAMS = 3
+PART = ROWS // STREAMS
+LAG = 1
+
+
+def feed_forward_kernel(
+    partial_ref, resid_ref, modulation_ref, up_ref, down_rows_ref, out_ref,
+    weights, other_pack, sib1, opposite, pairs, state, resid_rows, normed, hidden, down, sib2, ring,
+    local_sem, w_send, w_recv, s1_send, s1_recv, r1_send, r1_recv,
+    ag_send, ag_recv, agsib_send, agsib_recv, s2_send, s2_recv, r2_send, r2_recv,
+):
+    me = lax.axis_index("head")
+    frame = lax.axis_index("frame")
+    z_hi, core = me // 2, lax.rem(me, 2)
+    z_lo, yx = frame // 16, lax.rem(frame, 16)
+    y, x = yx // 4, lax.rem(yx, 4)
+    z = z_hi * 2 + z_lo
+    halves = (pl.ds(0, HALF), pl.ds(HALF, HALF))
+
+    def z_device(other):
+        return {"head": (other // 2) * 2 + core, "frame": lax.rem(other, 2) * 16 + yx}
+
+    sibling = {"head": z_hi * 2 + 1 - core, "frame": frame}
+    above, below = z_device(lax.rem(z + 1, 8)), z_device(lax.rem(z + 7, 8))
+    above2, below2 = z_device(lax.rem(z + 2, 8)), z_device(lax.rem(z + 6, 8))
+    x_peers = [{"head": me, "frame": z_lo * 16 + y * 4 + lax.rem(x + k, 4)} for k in (1, 2, 3)]
+    y_peers = [{"head": me, "frame": z_lo * 16 + lax.rem(y + k, 4) * 4 + x} for k in (1, 2, 3)]
+    other_plane = z_device(z + 1 - 2 * z_lo)
+
+    barrier = pltpu.get_barrier_semaphore()
+    greeted = [sibling, above, below, above2, below2] + x_peers + y_peers
+    for device in greeted:
+        pl.semaphore_signal(barrier, inc=1, device_id=device, device_id_type=MESH)
+
+    my_rows = pl.ds(pl.multiple_of(me * ROWS, 16), ROWS)
+    fetch_resid = pltpu.make_async_copy(resid_ref.at[my_rows], resid_rows, local_sem.at[0])
+    fetch_resid.start()
+
+    lane = lax.broadcasted_iota(jnp.int32, (WROWS, 128), 1)
+    blank = jnp.zeros((WROWS, 128 - 2 * TAIL), jnp.float32)
+    tails = [
+        jnp.concatenate([ref[:, 2 * MAIN:].astype(jnp.float32), blank], axis=1)
+        for ref in (up_ref, down_rows_ref)
+    ]
+    up_tail = [tails[0], pltpu.roll(tails[0], 128 - TAIL, 1)]
+    down_tail = [pltpu.roll(tails[1], TAIL, 1), tails[1]]
+    mixed_tail = []
+    for side in (0, 1):
+        down_part = jnp.where(lane < 2 * TAIL, down_tail[side], 0.0)
+        mixed_tail.append(jnp.where(lane < TAIL, up_tail[side], down_part))
+
+    def pack(target, side):
+        columns = pl.ds(pl.multiple_of(side * MAIN, 128), MAIN)
+        target[:, 0:MAIN] = up_ref[:, columns]
+        target[:, MAIN:512] = jnp.where(side == 0, mixed_tail[0], mixed_tail[1]).astype(jnp.bfloat16)
+        target[:, 512:PACK] = down_rows_ref[:, columns]
+
+    pack(other_pack, 1 - z_lo)
+    pack(weights.at[z_lo, y, x], z_lo)
+
+    pl.semaphore_wait(barrier, len(greeted))
+
+    started = []
+
+    def send(source, target, send_sem, recv_sem, device):
+        copy = pltpu.make_async_remote_copy(
+            source, target, send_sem, recv_sem, device_id=device, device_id_type=MESH
+        )
+        copy.start()
+        started.append(copy)
+        return copy
+
+    order = [lax.rem(z_hi + k, 4) for k in (2, 1, 3, 0)]
+    parts = [slice(r * PART, (r + 1) * PART) for r in range(STREAMS)]
+    s1 = [
+        [
+            send(
+                partial_ref.at[q, 1 - core, parts[r]], sib1.at[r, q],
+                s1_send.at[r, i], s1_recv.at[r, i], sibling,
+            )
+            for i, q in enumerate(order)
+        ]
+        for r in range(STREAMS)
+    ]
+
+    cross = send(other_pack, weights.at[z_lo, y, x], w_send.at[0], w_recv.at[0], other_plane)
+    first_a = [
+        send(
+            weights.at[z_lo, y, x], weights.at[z_lo, y, x],
+            w_send.at[1 + i], w_recv.at[1 + i], device,
+        )
+        for i, device in enumerate(x_peers)
+    ]
+    first_b, second = [], []
+
+    def weights_first():
+        cross.wait_recv()
+        view = weights.at[1 - z_lo, y, x]
+        for i, device in enumerate(y_peers):
+            first_b.append(send(view, view, w_send.at[4 + i], w_recv.at[4 + i], device))
+
+    def weights_second():
+        for copy in first_a:
+            copy.wait_recv()
+        view = weights.at[z_lo, y]
+        for i, device in enumerate(y_peers):
+            second.append(send(view, view, w_send.at[7 + i], w_recv.at[7 + i], device))
+        for copy in first_b:
+            copy.wait_recv()
+        view = weights.at[1 - z_lo, :, x]
+        for i, device in enumerate(x_peers):
+            second.append(send(view, view, w_send.at[10 + i], w_recv.at[10 + i], device))
+
+    def weights_here():
+        for copy in second:
+            copy.wait_recv()
+        second.clear()
+
+    def shard(distance):
+        return lax.rem(z + distance + 8, 8)
+
+    def up(r):
+        rows = normed[r].reshape(16 * PART, D)
+        total = None
+        for c in range(4):
+            weight = weights[c // 2, 2 * (c % 2):2 * (c % 2) + 2, :, :, 0:512].reshape(8 * WROWS, 512)
+            product = jnp.dot(
+                rows[:, c * 1280:(c + 1) * 1280], weight, preferred_element_type=jnp.float32
+            )
+            total = product if total is None else total + product
+        active = jax.nn.gelu(total, approximate=True)
+        place = lax.broadcasted_iota(jnp.int32, (16 * PART, 128), 1)
+        tail = pltpu.roll(active[:, MAIN:512], TAIL, 1)
+        tail = jnp.where((place >= TAIL) & (place < 2 * TAIL), tail, 0.0)
+        hidden[:, 0:128] = tail.astype(jnp.bfloat16)
+        hidden[:, 128:512] = active[:, 0:MAIN].astype(jnp.bfloat16)
+
+    def project(r):
+        def columns_of(c, carry):
+            weight = weights[c // 4, lax.rem(c, 4), :, :, MAIN:PACK].reshape(4 * WROWS, 512)
+            columns = pl.ds(pl.multiple_of(c * 4 * WROWS, 128), 4 * WROWS)
+            product = lax.dot_general(
+                hidden[...], weight, (((1,), (1,)), ((), ())), preferred_element_type=jnp.float32
+            )
+            down[r, :, :, :, columns] = product.astype(jnp.bfloat16).reshape(8, 2, PART, 4 * WROWS)
+            return carry
+
+        lax.fori_loop(0, 8, columns_of, 0)
+
+    def stream(r):
+        rows = parts[r]
+
+        def pair(q):
+            return partial_ref[q, core, rows].astype(jnp.float32) + sib1[r, q].astype(jnp.float32)
+
+        s1[r][0].wait_recv()
+        q = order[0]
+        sib1[r, q] = pair(q).astype(jnp.bfloat16)
+        opposites = [
+            send(
+                sib1.at[r, q, :, halves[way]], opposite.at[r, way],
+                r1_send.at[r, way], r1_recv.at[r, way], (above2, below2)[way],
+            )
+            for way in (0, 1)
+        ]
+        yield
+        finals = []
+        for way in (0, 1):
+            s1[r][1 + way].wait_recv()
+            opposites[way].wait_recv()
+            q = order[1 + way]
+            total = pair(q)
+            moved = total[:, way * HALF:(way + 1) * HALF] + opposite[r, way].astype(jnp.float32)
+            kept = total[:, (1 - way) * HALF:(2 - way) * HALF]
+            sib1[r, q, :, halves[way]] = moved.astype(jnp.bfloat16)
+            sib1[r, q, :, halves[1 - way]] = kept.astype(jnp.bfloat16)
+            finals.append(send(
+                sib1.at[r, q], pairs.at[r, way],
+                r1_send.at[r, 2 + way], r1_recv.at[r, 2 + way], (above2, below2)[way],
+            ))
+        yield
+        s1[r][3].wait_recv()
+        for copy in finals:
+            copy.wait_recv()
+        if r == 0:
+            fetch_resid.wait()
+        branch = (
+            pair(z_hi) + pairs[r, 0].astype(jnp.float32) + pairs[r, 1].astype(jnp.float32)
+        )
+        value = resid_rows[rows].astype(jnp.float32) + modulation_ref[0:1] * branch
+        state[r] = value
+        average = jnp.mean(value, axis=-1, keepdims=True)
+        centered = value - average
+        variance = jnp.mean(centered * centered, axis=-1, keepdims=True)
+        normal_form = centered * lax.rsqrt(variance + 1e-06)
+        normed[r, z, core] = (
+            normal_form * (1.0 + modulation_ref[2:3]) + modulation_ref[1:2]
+        ).astype(jnp.bfloat16)
+
+        gathered = []
+
+        def to_sibling(view, index):
+            gathered.append(send(
+                view, view, agsib_send.at[r, index], agsib_recv.at[r, index], sibling
+            ))
+
+        def hop(way, step):
+            view = normed.at[r, shard((1 - step) * (1 - 2 * way)), core]
+            if step == 4:
+                view = view.at[:, halves[way]]
+            return send(
+                view, view, ag_send.at[r, way, step - 1], ag_recv.at[r, way, step - 1],
+                (above, below)[way],
+            )
+
+        hops = [hop(0, 1), hop(1, 1)]
+        to_sibling(normed.at[r, z, core], 0)
+        yield
+        for step in (1, 2, 3, 4):
+            for way in (0, 1):
+                hops[way].wait_recv()
+                view = normed.at[r, shard(-step * (1 - 2 * way)), core]
+                if step < 4:
+                    hops[way] = hop(way, step + 1)
+                else:
+                    view = view.at[:, halves[way]]
+                to_sibling(view, 1 + (step - 1) * 2 + way)
+            yield
+        for copy in gathered:
+            copy.wait_recv()
+        weights_here()
+        up(r)
+        project(r)
+        s2 = {}
+        for i, distance in enumerate((4, 3, -3, 2, -2, 1, -1, 0)):
+            q = shard(distance)
+            s2[distance] = send(
+                down.at[r, q, 1 - core], sib2.at[r, q], s2_send.at[r, i], s2_recv.at[r, i], sibling
+            )
+        yield
+
+        def pair2(q):
+            return down[r, q, core].astype(jnp.float32) + sib2[r, q].astype(jnp.float32)
+
+        sums = [None, None]
+        for step in (1, 2, 3, 4):
+            for way in (0, 1):
+                distance = (5 - step) * (1 - 2 * way)
+                q = shard(distance)
+                if step == 1:
+                    if way == 0:
+                        s2[4].wait_recv()
+                        sib2[r, q] = pair2(q).astype(jnp.bfloat16)
+                    source = sib2.at[r, q, :, halves[way]]
+                    target = ring.at[r, way, 0, :, halves[way]]
+                else:
+                    s2[distance].wait_recv()
+                    total = pair2(q)
+                    sums[way].wait_recv()
+                    if step == 2:
+                        moved = (
+                            total[:, way * HALF:(way + 1) * HALF]
+                            + ring[r, way, 0, :, halves[way]].astype(jnp.float32)
+                        )
+                        kept = total[:, (1 - way) * HALF:(2 - way) * HALF]
+                        sib2[r, q, :, halves[way]] = moved.astype(jnp.bfloat16)
+                        sib2[r, q, :, halves[1 - way]] = kept.astype(jnp.bfloat16)
+                    else:
+                        total = total + ring[r, way, step - 2].astype(jnp.float32)
+                        sib2[r, q] = total.astype(jnp.bfloat16)
+                    source, target = sib2.at[r, q], ring.at[r, way, step - 1]
+                sums[way] = send(
+                    source, target, r2_send.at[r, way, step - 1], r2_recv.at[r, way, step - 1],
+                    (above, below)[way],
+                )
+            yield
+        s2[0].wait_recv()
+        ffn = pair2(z)
+        for way in (0, 1):
+            sums[way].wait_recv()
+            ffn = ffn + ring[r, way, 3].astype(jnp.float32)
+        out_ref[rows] = (state[r] + modulation_ref[3:4] * ffn).astype(jnp.bfloat16)
+        yield
+
+    stages = 13
+    streams = [stream(r) for r in range(STREAMS)]
+    for tick in range(stages + LAG * (STREAMS - 1)):
+        for r in range(STREAMS):
+            if 0 <= tick - LAG * r < stages:
+                next(streams[r])
+        if tick == 0:
+            weights_first()
+        if tick == 2:
+            weights_second()
+
+    for copy in started:
+        copy.wait_send()
+
+
+def feed_forward(partial_value, resid, modulation, up_weight, down_rows):
+    dma = pltpu.SemaphoreType.DMA
+    bf16 = jnp.bfloat16
+    return pl.pallas_call(
+        feed_forward_kernel,
+        out_shape=jax.ShapeDtypeStruct((ROWS, D), bf16),
+        in_specs=[
+            pl.BlockSpec(memory_space=pltpu.VMEM),
+            pl.BlockSpec(memory_space=pl.ANY),
+            pl.BlockSpec(memory_space=pltpu.VMEM),
+            pl.BlockSpec(memory_space=pltpu.VMEM),
+            pl.BlockSpec(memory_space=pltpu.VMEM),
+        ],
+        out_specs=pl.BlockSpec(memory_space=pltpu.VMEM),
+        scratch_shapes=[
+            pltpu.VMEM((2, 4, 4, WROWS, PACK), bf16),
+            pltpu.VMEM((WROWS, PACK), bf16),
+            pltpu.VMEM((STREAMS, 4, PART, D), bf16),
+            pltpu.VMEM((STREAMS, 2, PART, HALF), bf16),
+            pltpu.VMEM((STREAMS, 2, PART, D), bf16),
+            pltpu.VMEM((STREAMS, PART, D), jnp.float32),
+            pltpu.VMEM((ROWS, D), bf16),
+            pltpu.VMEM((STREAMS, 8, 2, PART, D), bf16),
+            pltpu.VMEM((16 * PART, 512), bf16),
+            pltpu.VMEM((STREAMS, 8, 2, PART, D), bf16),
+            pltpu.VMEM((STREAMS, 8, PART, D), bf16),
+            pltpu.VMEM((STREAMS, 2, 4, PART, D), bf16),
+            dma((1,)), dma((13,)), dma((13,)),
+            dma((STREAMS, 4)), dma((STREAMS, 4)), dma((STREAMS, 4)), dma((STREAMS, 4)),
+            dma((STREAMS, 2, 4)), dma((STREAMS, 2, 4)), dma((STREAMS, 9)), dma((STREAMS, 9)),
+            dma((STREAMS, 8)), dma((STREAMS, 8)), dma((STREAMS, 2, 4)), dma((STREAMS, 2, 4)),
+        ],
+        compiler_params=pltpu.CompilerParams(
+            collective_id=1, has_side_effects=True, vmem_limit_bytes=58 * MIB
+        ),
+        name="feed_forward",
+    )(partial_value, resid, modulation, up_weight, down_rows)
 
 
 def shards(resid, qkv, band, out_weight, modulation, up_weight, down_weight):
-    head_count = lax.axis_size("head")
-    head_index = lax.axis_index("head")
     partial_value = attention(jnp.transpose(qkv, (1, 0, 2)), band, out_weight)
-    rows_dev = BLOCK // head_count
-    first_row = head_index * rows_dev
-    branch = lax.psum(partial_value, "head").astype(jnp.float32)
-    residual_state = resid.astype(jnp.float32) + modulation[0] * branch
-    normed = modulate(residual_state, modulation[1], modulation[2])
-    state_rows = lax.dynamic_slice_in_dim(residual_state, first_row, rows_dev, 0)
-    projected = jnp.dot(
-        normed,
-        lax.all_gather(up_weight, "frame", axis=0, tiled=True),
-        preferred_element_type=jnp.float32,
+    return feed_forward(
+        partial_value.reshape(4, 2, ROWS, D), resid, modulation, up_weight, jnp.transpose(down_weight)
     )
-    hidden = jax.nn.gelu(projected, approximate=True).astype(jnp.bfloat16)
-    down_terms = rounded(
-        jnp.dot(
-            hidden,
-            lax.all_gather(down_weight, "frame", axis=1, tiled=True),
-            preferred_element_type=jnp.float32,
-        )
-    )
-    ffn_out = lax.psum_scatter(
-        down_terms.astype(jnp.bfloat16), "head", scatter_dimension=0, tiled=True
-    ).astype(jnp.float32)
-    return (state_rows + modulation[3] * ffn_out).astype(jnp.bfloat16)
 
 
 def solution(mesh):

time: 607 us -> 245 us (0.40)
  waiting for transfers between devices: 440 us -> 0 us
  Pallas kernels: 117 us -> 241 us
  matrix products: 22.3 us -> 0 us
  between operations: 14.9 us -> 0.02 us
  other arithmetic: 8.01 us -> 0 us
    all_gather x2 -> x0, waiting for transfers between devices: 241 us -> none  [the longest x1 173 us: shards(): lax.all_gather(down_weight, 'frame', axis=1, tiled=True)]
    pallas_call x0 -> x1, Pallas kernels: none -> 140 us  [feed_forward(): pl.pallas_call(feed_forward_kernel, out_shape=jax.ShapeDtypeStruct((ROWS,...]
    psum x1 -> x0, waiting for transfers between devices: 140 us -> none  [shards(): branch = lax.psum(partial_value, 'head').astype(jnp.float32)]
    reduce_scatter x1 -> x0, waiting for transfers between devices: 57.8 us -> none  [shards(): lax.psum_scatter(down_terms.astype(jnp.bfloat16), 'head', scatter_dimensi...]
    dot_general x1 -> x0, matrix products: 22.3 us -> none  [shards(): jnp.dot(hidden, lax.all_gather(down_weight, 'frame', axis=1, tiled=True),...]
    pallas_call x1, Pallas kernels: 117 us -> 101 us  [attention(): pl.pallas_call(attention_kernel, out_shape=jax.ShapeDtypeStruct((BLOCK, D...]
  transfers between devices with their start and end apart: 4 -> 0, of which waited for: 4 -> 0; matrix products, arithmetic and copies ran while one was open for 1% -> 0% of each run, Pallas kernels for 0% -> 0%
where the time goes in v3:
time: 245 us; the launch traced here: 243 us
  Pallas kernels  241 us (98%)
    pallas_call x1, Pallas kernels, feed_forward(): pl.pallas_call(feed_forward_kernel, out_shape=jax.ShapeDtypeStruct((ROWS,...  140 us
    pallas_call x1, Pallas kernels, attention(): pl.pallas_call(attention_kernel, out_shape=jax.ShapeDtypeStruct((BLOCK, D...  101 us

profile of v3, /device:TPU:32, one launch (start us, length us, event | category | flops | bytes accessed | tf_op | source)
XLA Modules:
  0.0 242.8 jit_solution(5124118544550650585)
XLA Ops:
  0.0 101.2 %attention.1 = bf16[384,5120]{1,0:T(8,128)(2,1)} custom-call(bf16[3,48,5120]{2,1,0:T(8,128)(2,1)} %bitcast.4, s32[1,9]{1,0:T(1,128)} %band_ref.1, bf16[640,5120]{1,0:T(8,128)(2,1)} %weight_ref.1), custom_call_target="tpu_custom_call" | custom-call | tf_op jit(solution)/shard_map/attention/pallas_call | solution.py:227
  101.2 139.8 %feed_forward.1 = bf16[48,5120]{1,0:T(8,128)(2,1)} custom-call(bf16[4,2,48,5120]{3,2,1,0:T(8,128)(2,1)} %bitcast.3, bf16[384,5120]{1,0:T(8,128)(2,1)} %resid_ref.1, f32[4,5120]{1,0:T(4,128)} %modulation_ref.1, bf16[160,864]{1,0:T(8,128)(2,1)} %up_ref.1, bf16[160,864]{1,0:T(8,128)(2,1)} %bitcast.5), custom_call_target="tpu_custom_call" | custom-call | tf_op jit(solution)/shard_map/feed_forward/pallas_call | solution.py:562
  241.0 1.8 copy.9

commit v4 on v3

v4 whole, which is shorter than its diff:
```python
import functools
import math

import jax
import jax.numpy as jnp
from jax import lax
from jax.experimental import pallas as pl
from jax.experimental.pallas import tpu as pltpu
from jax.sharding import PartitionSpec as P

HD = 128
SLOTS = 9
BLOCK = 384
NBLK = 32
N_HEAD = 8
ROWS = BLOCK // N_HEAD
GROUP = 5
INNER = GROUP * HD
D = 5120
MESH = pl.DeviceIdType.MESH
MIB = 2**20

partner_offsets = (0, -8, -4, -2, -1, 1, 2, 4, 8)
VIA = "via"
SLOT = {offset: slot for slot, offset in enumerate(partner_offsets)}
QUERY_ROWS = 128
SCALE_LOG2 = math.log2(math.e) / math.sqrt(HD)
HALF = D // 2
UNITS = 432
MAIN = 384
TAIL = UNITS - MAIN
PACK = 896
WROWS = 160
STREAMS = 3
PART = ROWS // STREAMS
LAG = 1


def layer_kernel(
    qkv_ref, band_ref, out_weight_ref, resid_ref, modulation_ref, up_ref, down_rows_ref, out_ref,
    heads, via, attended, partial_ref,
    weights, other_pack, sib1, opposite, pairs, state, resid_rows, normed, hidden, down, sib2, ring,
    a2a_send, a2a_recv, own_sem, halo_send, halo_recv, weight_sem,
    local_sem, w_send, w_recv, s1_send, s1_recv, r1_send, r1_recv,
    ag_send, ag_recv, agsib_send, agsib_recv, s2_send, s2_recv, r2_send, r2_recv,
):
    me = lax.axis_index("head")
    frame = lax.axis_index("frame")
    block = frame
    z_hi, core = me // 2, lax.rem(me, 2)
    z_lo, yx = frame // 16, lax.rem(frame, 16)
    y, x = yx // 4, lax.rem(yx, 4)
    z = z_hi * 2 + z_lo
    row_start = frame - x
    halves = (pl.ds(0, HALF), pl.ds(HALF, HALF))

    def z_device(other):
        return {"head": (other // 2) * 2 + core, "frame": lax.rem(other, 2) * 16 + yx}

    sibling = {"head": z_hi * 2 + 1 - core, "frame": frame}
    above, below = z_device(lax.rem(z + 1, 8)), z_device(lax.rem(z + 7, 8))
    above2, below2 = z_device(lax.rem(z + 2, 8)), z_device(lax.rem(z + 6, 8))
    x_peers = [{"head": me, "frame": z_lo * 16 + y * 4 + lax.rem(x + k, 4)} for k in (1, 2, 3)]
    y_peers = [{"head": me, "frame": z_lo * 16 + lax.rem(y + k, 4) * 4 + x} for k in (1, 2, 3)]
    other_plane = z_device(z + 1 - 2 * z_lo)

    barrier = pltpu.get_barrier_semaphore()
    greeted = [above, below] + x_peers + y_peers
    greeted += [{"head": lax.rem(me + k, N_HEAD), "frame": frame} for k in range(1, N_HEAD)]
    greeted += [{"head": me, "frame": lax.rem(frame + k, NBLK)} for k in (4, 12, 16, 20, NBLK - 4)]
    for device in greeted:
        pl.semaphore_signal(barrier, inc=1, device_id=device, device_id_type=MESH)

    my_rows = pl.ds(pl.multiple_of(me * ROWS, 16), ROWS)
    fetch_resid = pltpu.make_async_copy(resid_ref.at[my_rows], resid_rows, local_sem.at[0])
    fetch_resid.start()

    lane = lax.broadcasted_iota(jnp.int32, (WROWS, 128), 1)
    blank = jnp.zeros((WROWS, 128 - 2 * TAIL), jnp.float32)
    tails = [
        jnp.concatenate([ref[:, 2 * MAIN:].astype(jnp.float32), blank], axis=1)
        for ref in (up_ref, down_rows_ref)
    ]
    up_tail = [tails[0], pltpu.roll(tails[0], 128 - TAIL, 1)]
    down_tail = [pltpu.roll(tails[1], TAIL, 1), tails[1]]
    mixed_tail = []
    for side in (0, 1):
        down_part = jnp.where(lane < 2 * TAIL, down_tail[side], 0.0)
        mixed_tail.append(jnp.where(lane < TAIL, up_tail[side], down_part))

    def pack(target, side):
        columns = pl.ds(pl.multiple_of(side * MAIN, 128), MAIN)
        target[:, 0:MAIN] = up_ref[:, columns]
        target[:, MAIN:512] = jnp.where(side == 0, mixed_tail[0], mixed_tail[1]).astype(jnp.bfloat16)
        target[:, 512:PACK] = down_rows_ref[:, columns]

    pack(other_pack, 1 - z_lo)
    pack(weights.at[z_lo, y, x], z_lo)

    pl.semaphore_wait(barrier, len(greeted))

    def remote(source, target, send_sem, recv_sem, device):
        return pltpu.make_async_remote_copy(
            source, target, send_sem, recv_sem, device_id=device, device_id_type=MESH
        )

    own_view, other_view = weights.at[z_lo, y, x], weights.at[1 - z_lo, y, x]
    cross = remote(other_pack, own_view, w_send.at[0], w_recv.at[0], other_plane)
    right, left = lax.rem(x + 1, 4), lax.rem(x + 3, 4)
    front, back = lax.rem(y + 1, 4), lax.rem(y + 3, 4)
    to_right, to_left, to_front, to_back = x_peers[0], x_peers[2], y_peers[0], y_peers[2]
    upper, lower = pl.ds(0, WROWS // 2), pl.ds(WROWS // 2, WROWS // 2)
    low, high = pl.ds(0, 2), pl.ds(2, 2)

    def weight_hops(first, hops):
        return [
            remote(view, view, w_send.at[first + i], w_recv.at[first + i], device)
            for i, (view, device) in enumerate(hops)
        ]

    def row_part(row, part):
        return weights.at[z_lo, row, part]

    def column_part(column, part):
        return weights.at[1 - z_lo, part, column]

    piece_near = weight_hops(1, (
        (own_view, to_right), (own_view, to_left), (other_view, to_front), (other_view, to_back),
    ))
    piece_far = weight_hops(5, (
        (weights.at[z_lo, y, left, upper], to_right), (weights.at[z_lo, y, right, lower], to_left),
        (weights.at[1 - z_lo, back, x, upper], to_front), (weights.at[1 - z_lo, front, x, lower], to_back),
    ))
    line_first = weight_hops(9, (
        (row_part(y, low), to_front), (row_part(y, high), to_back),
        (column_part(x, low), to_right), (column_part(x, high), to_left),
    ))
    line_then = weight_hops(13, (
        (row_part(y, high), to_front), (row_part(y, low), to_back),
        (column_part(x, high), to_right), (column_part(x, low), to_left),
    ))
    line_far = weight_hops(17, (
        (row_part(back, low), to_front), (row_part(front, high), to_back),
        (column_part(left, low), to_right), (column_part(right, high), to_left),
    ))
    weight_copies = [cross] + piece_near + piece_far + line_first + line_then + line_far

    def weight_step(landed, sent):
        for copy in landed:
            copy.wait_recv()
        for copy in sent:
            copy.start()

    def frame_device(frame):
        return {"head": me, "frame": frame}

    def head_device(head):
        return {"head": head, "frame": block}

    fetch_weight = pltpu.make_async_copy(out_weight_ref, down.at[0:INNER // PART], weight_sem)

    def to_peer(j, k):
        peer = lax.rem(me + k, N_HEAD)
        columns = pl.ds(pl.multiple_of(peer * INNER + j * HD, HD), HD)
        return pltpu.make_async_remote_copy(
            qkv_ref.at[:, :, columns], heads.at[j, :, 0, my_rows],
            a2a_send.at[j, k - 1], a2a_recv.at[j, k - 1],
            device_id=head_device(peer), device_id_type=MESH,
        )

    def own_piece(j):
        columns = pl.ds(pl.multiple_of(me * INNER + j * HD, HD), HD)
        return pltpu.make_async_copy(
            qkv_ref.at[:, :, columns], heads.at[j, :, 0, my_rows], own_sem.at[j]
        )

    def send_heads(j, carry):
        for k in (4, 3, 5, 2, 6, 1, 7):
            to_peer(j, k).start()
        own_piece(j).start()
        return carry

    lax.fori_loop(0, 2, send_heads, 0)
    cross.start()
    fetch_weight.start()

    low4, high4 = block >= 4, block < NBLK - 4
    both = slice(1, 3)
    routes = (
        (1, 0, -4, block + 4, high4, both),
        (1, 0, 4, block - 4, low4, both),
        (1, 0, -1, block + 1, x < 3, both),
        (1, 0, 1, block - 1, x > 0, both),
        (2, -4, -8, block + 4, low4 & high4 & (block // 4 != 3), both),
        (2, 4, 8, block - 4, low4 & high4 & (block // 4 != 4), both),
        (2, -4, VIA, block - 12, block // 4 == 3, both),
        (2, 4, VIA, block + 12, block // 4 == 4, both),
        (3, VIA, -8, block + 16, block // 4 == 0, both),
        (3, VIA, 8, block - 16, block // 4 == 7, both),
        (2, -4, -1, row_start, (x == 3) & low4, both),
        (2, 4, 1, row_start + 3, (x == 0) & high4, both),
        (2, -1, -2, block + 1, (x == 1) | (x == 2), both),
        (2, 1, 2, block - 1, (x == 1) | (x == 2), both),
        (2, -4, -2, row_start, (x == 2) & low4, both),
        (2, 4, 2, row_start + 3, (x == 1) & high4, both),
        (3, -1, -2, block + 1, (x == 0) & low4, both),
        (3, 1, 2, block - 1, (x == 3) & high4, both),
    )
    arrivals = (
        (2, -4, low4, both),
        (2, 4, high4, both),
        (2, -1, x > 0, both),
        (2, 1, x < 3, both),
        (3, VIA, (block // 4 == 0) | (block // 4 == 7), both),
        (3, -1, (x == 0) & low4, both),
        (3, 1, (x == 3) & high4, both),
        (4, 2, block < NBLK - 2, both),
        (4, -2, block >= 2, both),
        (4, -8, block >= 8, both),
        (4, 8, block < NBLK - 8, both),
    )

    def place(j, slot, part):
        return via.at[j] if slot == VIA else heads.at[j, part, SLOT[slot]]

    def halo_sem(slot):
        return SLOTS - 1 if slot == VIA else SLOT[slot] - 1

    def route_copy(j, index):
        _, source, target, frame_to, _, part = routes[index]
        return pltpu.make_async_remote_copy(
            place(j, source, part), place(j, target, part),
            halo_send.at[j, index], halo_recv.at[j, halo_sem(target)],
            device_id=frame_device(jnp.clip(frame_to, 0, NBLK - 1)), device_id_type=MESH,
        )

    def send_stage(j, stage):
        for index, route in enumerate(routes):
            if route[0] == stage:
                @pl.when(route[4])
                def _():
                    route_copy(j, index).start()

    def wait_stage(j, stage):
        for before, slot, when, part in arrivals:
            if before == stage:
                @pl.when(when)
                def _():
                    landed = place(j, slot, part)
                    pltpu.make_async_copy(landed, landed, halo_recv.at[j, halo_sem(slot)]).wait()

    for offset in partner_offsets[1:]:
        partner = block + offset

        @pl.when((partner < 0) | (partner >= NBLK))
        def _():
            heads[:, 1:3, SLOT[offset]] = jnp.zeros((GROUP, 2, BLOCK, HD), jnp.bfloat16)

    def attend(j):
        widths = []
        for slot, offset in enumerate(partner_offsets):
            partner = block + offset
            present = (partner >= 0) & (partner < NBLK)
            widths.append(jnp.where(present, band_ref[0, slot], 0))
        keys = heads[j, 1].reshape(SLOTS * BLOCK, HD)
        values = heads[j, 2].reshape(SLOTS * BLOCK, HD)
        columns = pl.ds(pl.multiple_of(j * HD, HD), HD)
        for first in range(0, BLOCK, QUERY_ROWS):
            queries = heads[j, 0, 0, first:first + QUERY_ROWS]
            scores = lax.dot_general(
                queries, keys, (((1,), (1,)), ((), ())), preferred_element_type=jnp.float32
            )
            row = lax.broadcasted_iota(jnp.int32, (QUERY_ROWS, BLOCK), 0) + first
            column = lax.broadcasted_iota(jnp.int32, (QUERY_ROWS, BLOCK), 1)
            distance = jnp.abs(row - column)
            parts = []
            for slot in range(SLOTS):
                part = scores[:, slot * BLOCK:(slot + 1) * BLOCK]
                parts.append(jnp.where(distance < widths[slot], part, -1e30))
            top = functools.reduce(jnp.maximum, parts)
            row_max = jnp.max(top, axis=1, keepdims=True)
            weights = [jnp.exp2((part - row_max) * SCALE_LOG2) for part in parts]
            denominator = jnp.sum(functools.reduce(jnp.add, weights), axis=1, keepdims=True)
            probabilities = jnp.concatenate([w.astype(jnp.bfloat16) for w in weights], axis=1)
            summed = jnp.dot(probabilities, values, preferred_element_type=jnp.float32)
            attended[first:first + QUERY_ROWS, columns] = (summed / denominator).astype(jnp.bfloat16)

    def step(it, carry):
        @pl.when(it < GROUP)
        def _():
            for k in range(1, N_HEAD):
                origin = lax.rem(me + N_HEAD - k, N_HEAD)
                landed = heads.at[it, :, 0, pl.ds(pl.multiple_of(origin * ROWS, 16), ROWS)]
                pltpu.make_async_copy(landed, landed, a2a_recv.at[it, k - 1]).wait()
            own_piece(it).wait()
            send_stage(it, 1)

        @pl.when(it < GROUP - 2)
        def _():
            send_heads(it + 2, 0)

        @pl.when((it >= 1) & (it < GROUP + 1))
        def _():
            wait_stage(it - 1, 2)
            send_stage(it - 1, 2)

        @pl.when((it >= 2) & (it < GROUP + 2))
        def _():
            wait_stage(it - 2, 3)
            send_stage(it - 2, 3)

        @pl.when(it == GROUP + 2)
        def _():
            weight_step([cross], piece_near)

        @pl.when(it >= 3)
        def _():
            wait_stage(it - 3, 4)
            attend(it - 3)

        return carry

    lax.fori_loop(0, GROUP + 3, step, 0)

    fetch_weight.wait()

    started = []

    def send(source, target, send_sem, recv_sem, device):
        copy = pltpu.make_async_remote_copy(
            source, target, send_sem, recv_sem, device_id=device, device_id_type=MESH
        )
        copy.start()
        started.append(copy)
        return copy

    order = [lax.rem(z_hi + k, 4) for k in (2, 1, 3, 0)]
    parts = [slice(r * PART, (r + 1) * PART) for r in range(STREAMS)]
    s1 = []

    def project_heads(r):
        rows = attended[...].reshape(N_HEAD, STREAMS, PART, INNER)[:, r].reshape(N_HEAD * PART, INNER)

        def columns_of(c, carry):
            columns = pl.ds(pl.multiple_of(c * 512, 512), 512)
            weight = down[0:INNER // PART, :, columns].reshape(INNER, 512)
            product = jnp.dot(rows, weight, preferred_element_type=jnp.float32)
            partial_ref[r, :, :, :, columns] = product.astype(jnp.bfloat16).reshape(4, 2, PART, 512)
            return carry

        lax.fori_loop(0, D // 512, columns_of, 0)
        s1.append([
            send(
                partial_ref.at[r, q, 1 - core], sib1.at[r, q],
                s1_send.at[r, i], s1_recv.at[r, i], sibling,
            )
            for i, q in enumerate(order)
        ])

    def shard(distance):
        return lax.rem(z + distance + 8, 8)

    def up(r):
        rows = normed[r].reshape(16 * PART, D)
        total = None
        for c in range(4):
            weight = weights[c // 2, 2 * (c % 2):2 * (c % 2) + 2, :, :, 0:512].reshape(8 * WROWS, 512)
            product = jnp.dot(
                rows[:, c * 1280:(c + 1) * 1280], weight, preferred_element_type=jnp.float32
            )
            total = product if total is None else total + product
        active = jax.nn.gelu(total, approximate=True)
        place = lax.broadcasted_iota(jnp.int32, (16 * PART, 128), 1)
        tail = pltpu.roll(active[:, MAIN:512], TAIL, 1)
        tail = jnp.where((place >= TAIL) & (place < 2 * TAIL), tail, 0.0)
        hidden[:, 0:128] = tail.astype(jnp.bfloat16)
        hidden[:, 128:512] = active[:, 0:MAIN].astype(jnp.bfloat16)

    def project(r):
        def columns_of(c, carry):
            weight = weights[c // 4, lax.rem(c, 4), :, :, MAIN:PACK].reshape(4 * WROWS, 512)
            columns = pl.ds(pl.multiple_of(c * 4 * WROWS, 128), 4 * WROWS)
            product = lax.dot_general(
                hidden[...], weight, (((1,), (1,)), ((), ())), preferred_element_type=jnp.float32
            )
            down[r * 16:(r + 1) * 16, :, columns] = product.astype(jnp.bfloat16).reshape(16, PART, 4 * WROWS)
            return carry

        lax.fori_loop(0, 8, columns_of, 0)

    def stream(r):
        rows = parts[r]

        def pair(q):
            return partial_ref[r, q, core].astype(jnp.float32) + sib1[r, q].astype(jnp.float32)

        s1[r][0].wait_recv()
        q = order[0]
        sib1[r, q] = pair(q).astype(jnp.bfloat16)
        opposites = [
            send(
                sib1.at[r, q, :, halves[way]], opposite.at[r, way],
                r1_send.at[r, way], r1_recv.at[r, way], (above2, below2)[way],
            )
            for way in (0, 1)
        ]
        yield
        finals = []
        for way in (0, 1):
            s1[r][1 + way].wait_recv()
            opposites[way].wait_recv()
            q = order[1 + way]
            total = pair(q)
            moved = total[:, way * HALF:(way + 1) * HALF] + opposite[r, way].astype(jnp.float32)
            kept = total[:, (1 - way) * HALF:(2 - way) * HALF]
            sib1[r, q, :, halves[way]] = moved.astype(jnp.bfloat16)
            sib1[r, q, :, halves[1 - way]] = kept.astype(jnp.bfloat16)
            finals.append(send(
                sib1.at[r, q], pairs.at[r, way],
                r1_send.at[r, 2 + way], r1_recv.at[r, 2 + way], (above2, below2)[way],
            ))
        yield
        s1[r][3].wait_recv()
        for copy in finals:
            copy.wait_recv()
        if r == 0:
            fetch_resid.wait()
        branch = (
            pair(z_hi) + pairs[r, 0].astype(jnp.float32) + pairs[r, 1].astype(jnp.float32)
        )
        value = resid_rows[rows].astype(jnp.float32) + modulation_ref[0:1] * branch
        state[r] = value
        average = jnp.mean(value, axis=-1, keepdims=True)
        centered = value - average
        variance = jnp.mean(centered * centered, axis=-1, keepdims=True)
        normal_form = centered * lax.rsqrt(variance + 1e-06)
        normed[r, z, core] = (
            normal_form * (1.0 + modulation_ref[2:3]) + modulation_ref[1:2]
        ).astype(jnp.bfloat16)

        gathered = []

        def to_sibling(view, index):
            gathered.append(send(
                view, view, agsib_send.at[r, index], agsib_recv.at[r, index], sibling
            ))

        def hop(way, step):
            view = normed.at[r, shard((1 - step) * (1 - 2 * way)), core]
            if step == 4:
                view = view.at[:, halves[way]]
            return send(
                view, view, ag_send.at[r, way, step - 1], ag_recv.at[r, way, step - 1],
                (above, below)[way],
            )

        hops = [hop(0, 1), hop(1, 1)]
        to_sibling(normed.at[r, z, core], 0)
        yield
        for step in (1, 2, 3, 4):
            for way in (0, 1):
                hops[way].wait_recv()
                view = normed.at[r, shard(-step * (1 - 2 * way)), core]
                if step < 4:
                    hops[way] = hop(way, step + 1)
                else:
                    view = view.at[:, halves[way]]
                to_sibling(view, 1 + (step - 1) * 2 + way)
            yield
        for copy in gathered:
            copy.wait_recv()
        if r == 0:
            weight_step(line_then + line_far, [])
        up(r)
        project(r)
        s2 = {}
        for i, distance in enumerate((4, 3, -3, 2, -2, 1, -1, 0)):
            q = shard(distance)
            s2[distance] = send(
                down.at[r * 16 + q * 2 + 1 - core], sib2.at[r, q], s2_send.at[r, i], s2_recv.at[r, i], sibling
            )
        yield

        def pair2(q):
            return down[r * 16 + q * 2 + core].astype(jnp.float32) + sib2[r, q].astype(jnp.float32)

        sums = [None, None]
        for step in (1, 2, 3, 4):
            for way in (0, 1):
                distance = (5 - step) * (1 - 2 * way)
                q = shard(distance)
                if step == 1:
                    if way == 0:
                        s2[4].wait_recv()
                        sib2[r, q] = pair2(q).astype(jnp.bfloat16)
                    source = sib2.at[r, q, :, halves[way]]
                    target = ring.at[r, way, 0, :, halves[way]]
                else:
                    s2[distance].wait_recv()
                    total = pair2(q)
                    sums[way].wait_recv()
                    if step == 2:
                        moved = (
                            total[:, way * HALF:(way + 1) * HALF]
                            + ring[r, way, 0, :, halves[way]].astype(jnp.float32)
                        )
                        kept = total[:, (1 - way) * HALF:(2 - way) * HALF]
                        sib2[r, q, :, halves[way]] = moved.astype(jnp.bfloat16)
                        sib2[r, q, :, halves[1 - way]] = kept.astype(jnp.bfloat16)
                    else:
                        total = total + ring[r, way, step - 2].astype(jnp.float32)
                        sib2[r, q] = total.astype(jnp.bfloat16)
                    source, target = sib2.at[r, q], ring.at[r, way, step - 1]
                sums[way] = send(
                    source, target, r2_send.at[r, way, step - 1], r2_recv.at[r, way, step - 1],
                    (above, below)[way],
                )
            yield
        s2[0].wait_recv()
        ffn = pair2(z)
        for way in (0, 1):
            sums[way].wait_recv()
            ffn = ffn + ring[r, way, 3].astype(jnp.float32)
        out_ref[rows] = (state[r] + modulation_ref[3:4] * ffn).astype(jnp.bfloat16)
        yield

    stages = 13
    streams = [stream(r) for r in range(STREAMS)]
    weight_step(piece_near, piece_far)
    project_heads(0)
    project_heads(1)
    weight_step(piece_far, line_first + line_then)
    for tick in range(stages + LAG * (STREAMS - 1)):
        for r in range(STREAMS):
            if 0 <= tick - LAG * r < stages:
                next(streams[r])
        if tick == 0:
            project_heads(2)
        if tick == 2:
            weight_step(line_first, line_far)

    for copy in started + weight_copies:
        copy.wait_send()
    def finish(j, carry):
        for k in range(1, N_HEAD):
            to_peer(j, k).wait_send()
        for index, route in enumerate(routes):
            @pl.when(route[4])
            def _():
                route_copy(j, index).wait_send()
        return carry

    lax.fori_loop(0, GROUP, finish, 0)


def layer(qkv, band, out_weight, resid, modulation, up_weight, down_rows):
    dma = pltpu.SemaphoreType.DMA
    bf16 = jnp.bfloat16
    anywhere, vmem = pl.BlockSpec(memory_space=pl.ANY), pl.BlockSpec(memory_space=pltpu.VMEM)
    return pl.pallas_call(
        layer_kernel,
        out_shape=jax.ShapeDtypeStruct((ROWS, D), bf16),
        in_specs=[
            anywhere, pl.BlockSpec(memory_space=pltpu.SMEM), anywhere, anywhere, vmem, vmem, vmem,
        ],
        out_specs=vmem,
        scratch_shapes=[
            pltpu.VMEM((GROUP, 3, SLOTS, BLOCK, HD), bf16),
            pltpu.VMEM((GROUP, 2, BLOCK, HD), bf16),
            pltpu.VMEM((BLOCK, INNER), bf16),
            pltpu.VMEM((STREAMS, 4, 2, PART, D), bf16),
            pltpu.VMEM((2, 4, 4, WROWS, PACK), bf16),
            pltpu.VMEM((WROWS, PACK), bf16),
            pltpu.VMEM((STREAMS, 4, PART, D), bf16),
            pltpu.VMEM((STREAMS, 2, PART, HALF), bf16),
            pltpu.VMEM((STREAMS, 2, PART, D), bf16),
            pltpu.VMEM((STREAMS, PART, D), jnp.float32),
            pltpu.VMEM((ROWS, D), bf16),
            pltpu.VMEM((STREAMS, 8, 2, PART, D), bf16),
            pltpu.VMEM((16 * PART, 512), bf16),
            pltpu.VMEM((STREAMS * 16, PART, D), bf16),
            pltpu.VMEM((STREAMS, 8, PART, D), bf16),
            pltpu.VMEM((STREAMS, 2, 4, PART, D), bf16),
            dma((GROUP, N_HEAD - 1)), dma((GROUP, N_HEAD - 1)), dma((GROUP,)),
            dma((GROUP, 18)), dma((GROUP, SLOTS)), dma,
            dma((1,)), dma((21,)), dma((21,)),
            dma((STREAMS, 4)), dma((STREAMS, 4)), dma((STREAMS, 4)), dma((STREAMS, 4)),
            dma((STREAMS, 2, 4)), dma((STREAMS, 2, 4)), dma((STREAMS, 9)), dma((STREAMS, 9)),
            dma((STREAMS, 8)), dma((STREAMS, 8)), dma((STREAMS, 2, 4)), dma((STREAMS, 2, 4)),
        ],
        compiler_params=pltpu.CompilerParams(
            collective_id=0, has_side_effects=True, vmem_limit_bytes=62 * MIB
        ),
        name="layer",
    )(qkv, band, out_weight, resid, modulation, up_weight, down_rows)


def shards(resid, qkv, band, out_weight, modulation, up_weight, down_weight):
    return layer(
        jnp.transpose(qkv, (1, 0, 2)), band, out_weight.reshape(INNER // PART, PART, D),
        resid, modulation, up_weight, jnp.transpose(down_weight),
    )


def solution(mesh):
    in_specs = (
        P("frame", None),
        P(("frame", "head"), None, None),
        P("frame", None),
        P("head", None),
        P(),
        P("frame", "head"),
        P("head", "frame"),
    )
    out_specs = P(("frame", "head"), None)
    return jax.shard_map(shards, mesh=mesh, in_specs=in_specs, out_specs=out_specs, check_vma=False)
```

time: 245 us -> 235 us (0.959)
  Pallas kernels: 241 us -> 233 us
    pallas_call x2 -> x1, Pallas kernels: 241 us -> 233 us  [layer(): pl.pallas_call(layer_kernel, out_shape=jax.ShapeDtypeStruct((ROWS, D), bf...]
where the time goes in v4:
time: 235 us
  Pallas kernels  233 us (99%)
    pallas_call x1, Pallas kernels, layer(): pl.pallas_call(layer_kernel, out_shape=jax.ShapeDtypeStruct((ROWS, D), bf...  233 us

profile of v4, /device:TPU:32, one launch (start us, length us, event | category | flops | bytes accessed | tf_op | source)
XLA Modules:
  0.0 234.7 jit_solution(3463043095445948961)
XLA Ops:
  0.0 232.8 %layer.1 = bf16[48,5120]{1,0:T(8,128)(2,1)} custom-call(bf16[3,48,5120]{2,1,0:T(8,128)(2,1)} %bitcast.4, s32[1,9]{1,0:T(1,128)} %band_ref.1, bf16[40,16,5120]{2,1,0:T(8,128)(2,1)} %bitcast.3, bf16[384,5120]{1,0:T(8,128)(2,1)} %resid_ref.1, f32[4,5120]{1,0:T(4,128)} %modulation_ref.1, bf16[160,864]{1,0:T(8,128)(2,1)} %up_ref.1, bf16[160,864]{1,0:T(8,128)(2,1)} %bitcast.5), custom_call_target="tpu_custom_call" | custom-call | tf_op jit(solution)/shard_map/layer/pallas_call | solution.py:560
  232.8 1.8 copy.9

commit v5 on v4

--- a/solution.py
+++ b/solution.py
@@ -33,7 +33,7 @@
 WROWS = 160
 STREAMS = 3
 PART = ROWS // STREAMS
-LAG = 1
+LAG = 2
 
 
 def layer_kernel(
@@ -181,11 +181,12 @@
         return carry
 
     lax.fori_loop(0, 2, send_heads, 0)
-    cross.start()
+    for copy in [cross] + piece_near[:2]:
+        copy.start()
     fetch_weight.start()
 
     low4, high4 = block >= 4, block < NBLK - 4
-    both = slice(1, 3)
+    both, keys_only, values_only = slice(1, 3), slice(1, 2), slice(2, 3)
     routes = (
         (1, 0, -4, block + 4, high4, both),
         (1, 0, 4, block - 4, low4, both),
@@ -201,10 +202,12 @@
         (2, 4, 1, row_start + 3, (x == 0) & high4, both),
         (2, -1, -2, block + 1, (x == 1) | (x == 2), both),
         (2, 1, 2, block - 1, (x == 1) | (x == 2), both),
-        (2, -4, -2, row_start, (x == 2) & low4, both),
-        (2, 4, 2, row_start + 3, (x == 1) & high4, both),
+        (2, -4, -2, row_start, (x == 2) & low4, keys_only),
+        (2, 4, 2, row_start + 3, (x == 1) & high4, keys_only),
         (3, -1, -2, block + 1, (x == 0) & low4, both),
         (3, 1, 2, block - 1, (x == 3) & high4, both),
+        (3, 2, -2, block + 4, (x == 0) & high4, values_only),
+        (3, -2, 2, block - 4, (x == 3) & low4, values_only),
     )
     arrivals = (
         (2, -4, low4, both),
@@ -214,8 +217,14 @@
         (3, VIA, (block // 4 == 0) | (block // 4 == 7), both),
         (3, -1, (x == 0) & low4, both),
         (3, 1, (x == 3) & high4, both),
-        (4, 2, block < NBLK - 2, both),
-        (4, -2, block >= 2, both),
+        (3, 2, x == 0, both),
+        (3, -2, x == 3, both),
+        (4, 2, (x != 0) & (x != 3) & (block < NBLK - 2), both),
+        (4, -2, (x != 0) & (x != 3) & (block >= 2), both),
+        (4, -2, (x == 0) & low4, keys_only),
+        (4, -2, (x == 0) & low4, values_only),
+        (4, 2, (x == 3) & high4, keys_only),
+        (4, 2, (x == 3) & high4, values_only),
         (4, -8, block >= 8, both),
         (4, 8, block < NBLK - 8, both),
     )
@@ -223,14 +232,16 @@
     def place(j, slot, part):
         return via.at[j] if slot == VIA else heads.at[j, part, SLOT[slot]]
 
-    def halo_sem(slot):
+    def halo_sem(slot, part):
+        if part is values_only:
+            return SLOTS + (slot > 0)
         return SLOTS - 1 if slot == VIA else SLOT[slot] - 1
 
     def route_copy(j, index):
         _, source, target, frame_to, _, part = routes[index]
         return pltpu.make_async_remote_copy(
             place(j, source, part), place(j, target, part),
-            halo_send.at[j, index], halo_recv.at[j, halo_sem(target)],
+            halo_send.at[j, index], halo_recv.at[j, halo_sem(target, part)],
             device_id=frame_device(jnp.clip(frame_to, 0, NBLK - 1)), device_id_type=MESH,
         )
 
@@ -247,7 +258,7 @@
                 @pl.when(when)
                 def _():
                     landed = place(j, slot, part)
-                    pltpu.make_async_copy(landed, landed, halo_recv.at[j, halo_sem(slot)]).wait()
+                    pltpu.make_async_copy(landed, landed, halo_recv.at[j, halo_sem(slot, part)]).wait()
 
     for offset in partner_offsets[1:]:
         partner = block + offset
@@ -309,9 +320,17 @@
             wait_stage(it - 2, 3)
             send_stage(it - 2, 3)
 
+        @pl.when(it == 1)
+        def _():
+            weight_step([cross], piece_near[2:])
+
+        @pl.when(it == 2)
+        def _():
+            weight_step(piece_near, piece_far)
+
         @pl.when(it == GROUP + 2)
         def _():
-            weight_step([cross], piece_near)
+            weight_step(piece_far, line_first + line_then)
 
         @pl.when(it >= 3)
         def _():
@@ -445,25 +464,30 @@
                 view, view, agsib_send.at[r, index], agsib_recv.at[r, index], sibling
             ))
 
-        def hop(way, step):
-            view = normed.at[r, shard((1 - step) * (1 - 2 * way)), core]
-            if step == 4:
-                view = view.at[:, halves[way]]
-            return send(
-                view, view, ag_send.at[r, way, step - 1], ag_recv.at[r, way, step - 1],
+        hops = {}
+
+        def hop(way, step, half):
+            view = normed.at[r, shard((1 - step) * (1 - 2 * way)), core, :, halves[half]]
+            hops[way, half] = send(
+                view, view, ag_send.at[r, way, step - 1, half], ag_recv.at[r, way, step - 1, half],
                 (above, below)[way],
             )
 
-        hops = [hop(0, 1), hop(1, 1)]
+        for half in (0, 1):
+            for way in (0, 1):
+                hop(way, 1, half)
         to_sibling(normed.at[r, z, core], 0)
         yield
         for step in (1, 2, 3, 4):
+            for half in (0, 1):
+                for way in (0, 1):
+                    if step < 4 or half == way:
+                        hops[way, half].wait_recv()
+                    if step < 3 or step == 3 and half == way:
+                        hop(way, step + 1, half)
             for way in (0, 1):
-                hops[way].wait_recv()
                 view = normed.at[r, shard(-step * (1 - 2 * way)), core]
-                if step < 4:
-                    hops[way] = hop(way, step + 1)
-                else:
+                if step == 4:
                     view = view.at[:, halves[way]]
                 to_sibling(view, 1 + (step - 1) * 2 + way)
             yield
@@ -481,62 +505,59 @@
             )
         yield
 
-        def pair2(q):
-            return down[r * 16 + q * 2 + core].astype(jnp.float32) + sib2[r, q].astype(jnp.float32)
-
-        sums = [None, None]
+        def pair2(q, columns):
+            return (
+                down[r * 16 + q * 2 + core, :, columns].astype(jnp.float32)
+                + sib2[r, q, :, columns].astype(jnp.float32)
+            )
+
+        sums = {}
         for step in (1, 2, 3, 4):
             for way in (0, 1):
-                distance = (5 - step) * (1 - 2 * way)
-                q = shard(distance)
-                if step == 1:
-                    if way == 0:
-                        s2[4].wait_recv()
-                        sib2[r, q] = pair2(q).astype(jnp.bfloat16)
-                    source = sib2.at[r, q, :, halves[way]]
-                    target = ring.at[r, way, 0, :, halves[way]]
-                else:
-                    s2[distance].wait_recv()
-                    total = pair2(q)
-                    sums[way].wait_recv()
-                    if step == 2:
-                        moved = (
-                            total[:, way * HALF:(way + 1) * HALF]
-                            + ring[r, way, 0, :, halves[way]].astype(jnp.float32)
-                        )
-                        kept = total[:, (1 - way) * HALF:(2 - way) * HALF]
-                        sib2[r, q, :, halves[way]] = moved.astype(jnp.bfloat16)
-                        sib2[r, q, :, halves[1 - way]] = kept.astype(jnp.bfloat16)
-                    else:
-                        total = total + ring[r, way, step - 2].astype(jnp.float32)
-                        sib2[r, q] = total.astype(jnp.bfloat16)
-                    source, target = sib2.at[r, q], ring.at[r, way, step - 1]
-                sums[way] = send(
-                    source, target, r2_send.at[r, way, step - 1], r2_recv.at[r, way, step - 1],
-                    (above, below)[way],
-                )
+                if step > 1:
+                    s2[(5 - step) * (1 - 2 * way)].wait_recv()
+                elif way == 0:
+                    s2[4].wait_recv()
+            for turn in (0, 1):
+                for way in (0, 1):
+                    half = way if turn else 1 - way
+                    if step == 1 and not turn:
+                        continue
+                    q, columns = shard((5 - step) * (1 - 2 * way)), halves[half]
+                    total = pair2(q, columns)
+                    if (way, half) in sums:
+                        sums[way, half].wait_recv()
+                        total = total + ring[r, way, step - 2, :, columns].astype(jnp.float32)
+                    sib2[r, q, :, columns] = total.astype(jnp.bfloat16)
+                    sums[way, half] = send(
+                        sib2.at[r, q, :, columns], ring.at[r, way, step - 1, :, columns],
+                        r2_send.at[r, way, step - 1, half], r2_recv.at[r, way, step - 1, half],
+                        (above, below)[way],
+                    )
             yield
         s2[0].wait_recv()
-        ffn = pair2(z)
-        for way in (0, 1):
-            sums[way].wait_recv()
-            ffn = ffn + ring[r, way, 3].astype(jnp.float32)
-        out_ref[rows] = (state[r] + modulation_ref[3:4] * ffn).astype(jnp.bfloat16)
+        for half in (0, 1):
+            columns = halves[half]
+            ffn = pair2(z, columns)
+            for way in (0, 1):
+                sums[way, half].wait_recv()
+                ffn = ffn + ring[r, way, 3, :, columns].astype(jnp.float32)
+            out_ref[rows, columns] = (
+                state[r, :, columns] + modulation_ref[3:4, columns] * ffn
+            ).astype(jnp.bfloat16)
         yield
 
     stages = 13
     streams = [stream(r) for r in range(STREAMS)]
-    weight_step(piece_near, piece_far)
     project_heads(0)
     project_heads(1)
-    weight_step(piece_far, line_first + line_then)
     for tick in range(stages + LAG * (STREAMS - 1)):
         for r in range(STREAMS):
             if 0 <= tick - LAG * r < stages:
                 next(streams[r])
         if tick == 0:
             project_heads(2)
-        if tick == 2:
+        if tick == 0:
             weight_step(line_first, line_far)
 
     for copy in started + weight_copies:
@@ -582,11 +603,11 @@
             pltpu.VMEM((STREAMS, 8, PART, D), bf16),
             pltpu.VMEM((STREAMS, 2, 4, PART, D), bf16),
             dma((GROUP, N_HEAD - 1)), dma((GROUP, N_HEAD - 1)), dma((GROUP,)),
-            dma((GROUP, 18)), dma((GROUP, SLOTS)), dma,
+            dma((GROUP, 20)), dma((GROUP, SLOTS + 2)), dma,
             dma((1,)), dma((21,)), dma((21,)),
             dma((STREAMS, 4)), dma((STREAMS, 4)), dma((STREAMS, 4)), dma((STREAMS, 4)),
-            dma((STREAMS, 2, 4)), dma((STREAMS, 2, 4)), dma((STREAMS, 9)), dma((STREAMS, 9)),
-            dma((STREAMS, 8)), dma((STREAMS, 8)), dma((STREAMS, 2, 4)), dma((STREAMS, 2, 4)),
+            dma((STREAMS, 2, 4, 2)), dma((STREAMS, 2, 4, 2)), dma((STREAMS, 9)), dma((STREAMS, 9)),
+            dma((STREAMS, 8)), dma((STREAMS, 8)), dma((STREAMS, 2, 4, 2)), dma((STREAMS, 2, 4, 2)),
         ],
         compiler_params=pltpu.CompilerParams(
             collective_id=0, has_side_effects=True, vmem_limit_bytes=62 * MIB

time: 235 us -> 228 us (0.970); the launches traced: 235 us -> 224 us
  Pallas kernels: 233 us -> 222 us
    pallas_call x1, Pallas kernels: 233 us -> 222 us  [layer(): pl.pallas_call(layer_kernel, out_shape=jax.ShapeDtypeStruct((ROWS, D), bf...]
where the time goes in v5:
time: 228 us; the launch traced here: 224 us
  Pallas kernels  222 us (97%)
    pallas_call x1, Pallas kernels, layer(): pl.pallas_call(layer_kernel, out_shape=jax.ShapeDtypeStruct((ROWS, D), bf...  222 us

profile of v5, /device:TPU:32, one launch (start us, length us, event | category | flops | bytes accessed | tf_op | source)
XLA Modules:
  0.0 224.1 jit_solution(15428644142564080012)
XLA Ops:
  0.0 222.3 %layer.1 = bf16[48,5120]{1,0:T(8,128)(2,1)} custom-call(bf16[3,48,5120]{2,1,0:T(8,128)(2,1)} %bitcast.4, s32[1,9]{1,0:T(1,128)} %band_ref.1, bf16[40,16,5120]{2,1,0:T(8,128)(2,1)} %bitcast.3, bf16[384,5120]{1,0:T(8,128)(2,1)} %resid_ref.1, f32[4,5120]{1,0:T(4,128)} %modulation_ref.1, bf16[160,864]{1,0:T(8,128)(2,1)} %up_ref.1, bf16[160,864]{1,0:T(8,128)(2,1)} %bitcast.5), custom_call_target="tpu_custom_call" | custom-call | tf_op jit(solution)/shard_map/layer/pallas_call | solution.py:581
  222.3 1.8 copy.9

commit v6 on v5

--- a/solution.py
+++ b/solution.py
@@ -159,14 +159,23 @@
 
     fetch_weight = pltpu.make_async_copy(out_weight_ref, down.at[0:INNER // PART], weight_sem)
 
-    def to_peer(j, k):
+    queries_part, halo_part = slice(0, 1), slice(1, 3)
+
+    def to_peer(j, k, part):
         peer = lax.rem(me + k, N_HEAD)
         columns = pl.ds(pl.multiple_of(peer * INNER + j * HD, HD), HD)
+        kind = part.start
         return pltpu.make_async_remote_copy(
-            qkv_ref.at[:, :, columns], heads.at[j, :, 0, my_rows],
-            a2a_send.at[j, k - 1], a2a_recv.at[j, k - 1],
+            qkv_ref.at[part, :, columns], heads.at[j, part, 0, my_rows],
+            a2a_send.at[j, k - 1, kind], a2a_recv.at[j, k - 1, kind],
             device_id=head_device(peer), device_id_type=MESH,
         )
+
+    def wait_peers(j, part):
+        for k in range(1, N_HEAD):
+            origin = lax.rem(me + N_HEAD - k, N_HEAD)
+            landed = heads.at[j, part, 0, pl.ds(pl.multiple_of(origin * ROWS, 16), ROWS)]
+            pltpu.make_async_copy(landed, landed, a2a_recv.at[j, k - 1, part.start]).wait()
 
     def own_piece(j):
         columns = pl.ds(pl.multiple_of(me * INNER + j * HD, HD), HD)
@@ -176,9 +185,13 @@
 
     def send_heads(j, carry):
         for k in (4, 3, 5, 2, 6, 1, 7):
-            to_peer(j, k).start()
+            to_peer(j, k, halo_part).start()
         own_piece(j).start()
         return carry
+
+    def send_queries(j):
+        for k in (4, 3, 5, 2, 6, 1, 7):
+            to_peer(j, k, queries_part).start()
 
     lax.fori_loop(0, 2, send_heads, 0)
     for copy in [cross] + piece_near[:2]:
@@ -299,10 +312,7 @@
     def step(it, carry):
         @pl.when(it < GROUP)
         def _():
-            for k in range(1, N_HEAD):
-                origin = lax.rem(me + N_HEAD - k, N_HEAD)
-                landed = heads.at[it, :, 0, pl.ds(pl.multiple_of(origin * ROWS, 16), ROWS)]
-                pltpu.make_async_copy(landed, landed, a2a_recv.at[it, k - 1]).wait()
+            wait_peers(it, halo_part)
             own_piece(it).wait()
             send_stage(it, 1)
 
@@ -310,6 +320,10 @@
         def _():
             send_heads(it + 2, 0)
 
+        @pl.when(it < GROUP)
+        def _():
+            send_queries(it)
+
         @pl.when((it >= 1) & (it < GROUP + 1))
         def _():
             wait_stage(it - 1, 2)
@@ -330,10 +344,11 @@
 
         @pl.when(it == GROUP + 2)
         def _():
-            weight_step(piece_far, line_first + line_then)
+            weight_step(piece_far, [])
 
         @pl.when(it >= 3)
         def _():
+            wait_peers(it - 3, queries_part)
             wait_stage(it - 3, 4)
             attend(it - 3)
 
@@ -551,20 +566,22 @@
     streams = [stream(r) for r in range(STREAMS)]
     project_heads(0)
     project_heads(1)
+    weight_step([], line_first + line_then)
     for tick in range(stages + LAG * (STREAMS - 1)):
         for r in range(STREAMS):
             if 0 <= tick - LAG * r < stages:
                 next(streams[r])
         if tick == 0:
             project_heads(2)
-        if tick == 0:
+        if tick == 2:
             weight_step(line_first, line_far)
 
     for copy in started + weight_copies:
         copy.wait_send()
     def finish(j, carry):
         for k in range(1, N_HEAD):
-            to_peer(j, k).wait_send()
+            to_peer(j, k, queries_part).wait_send()
+            to_peer(j, k, halo_part).wait_send()
         for index, route in enumerate(routes):
             @pl.when(route[4])
             def _():
@@ -602,7 +619,7 @@
             pltpu.VMEM((STREAMS * 16, PART, D), bf16),
             pltpu.VMEM((STREAMS, 8, PART, D), bf16),
             pltpu.VMEM((STREAMS, 2, 4, PART, D), bf16),
-            dma((GROUP, N_HEAD - 1)), dma((GROUP, N_HEAD - 1)), dma((GROUP,)),
+            dma((GROUP, N_HEAD - 1, 2)), dma((GROUP, N_HEAD - 1, 2)), dma((GROUP,)),
             dma((GROUP, 20)), dma((GROUP, SLOTS + 2)), dma,
             dma((1,)), dma((21,)), dma((21,)),
             dma((STREAMS, 4)), dma((STREAMS, 4)), dma((STREAMS, 4)), dma((STREAMS, 4)),

time: 228 us -> 221 us (0.969)
  Pallas kernels: 222 us -> 215 us
    pallas_call x1, Pallas kernels: 222 us -> 215 us  [layer(): pl.pallas_call(layer_kernel, out_shape=jax.ShapeDtypeStruct((ROWS, D), bf...]
where the time goes in v6:
time: 221 us; the launch traced here: 216 us
  Pallas kernels  215 us (97%)
    pallas_call x1, Pallas kernels, layer(): pl.pallas_call(layer_kernel, out_shape=jax.ShapeDtypeStruct((ROWS, D), bf...  215 us

profile of v6, /device:TPU:32, one launch (start us, length us, event | category | flops | bytes accessed | tf_op | source)
XLA Modules:
  0.0 216.5 jit_solution(4596919305285852563)
XLA Ops:
  0.0 214.6 %layer.1 = bf16[48,5120]{1,0:T(8,128)(2,1)} custom-call(bf16[3,48,5120]{2,1,0:T(8,128)(2,1)} %bitcast.4, s32[1,9]{1,0:T(1,128)} %band_ref.1, bf16[40,16,5120]{2,1,0:T(8,128)(2,1)} %bitcast.3, bf16[384,5120]{1,0:T(8,128)(2,1)} %resid_ref.1, f32[4,5120]{1,0:T(4,128)} %modulation_ref.1, bf16[160,864]{1,0:T(8,128)(2,1)} %up_ref.1, bf16[160,864]{1,0:T(8,128)(2,1)} %bitcast.5), custom_call_target="tpu_custom_call" | custom-call | tf_op jit(solution)/shard_map/layer/pallas_call | solution.py:598
  214.6 1.8 copy.9

commit v7 on v6

--- a/solution.py
+++ b/solution.py
@@ -194,7 +194,7 @@
             to_peer(j, k, queries_part).start()
 
     lax.fori_loop(0, 2, send_heads, 0)
-    for copy in [cross] + piece_near[:2]:
+    for copy in piece_near[:2]:
         copy.start()
     fetch_weight.start()
 
@@ -336,9 +336,13 @@
 
         @pl.when(it == 1)
         def _():
+            weight_step([], [cross])
+
+        @pl.when(it == 3)
+        def _():
             weight_step([cross], piece_near[2:])
 
-        @pl.when(it == 2)
+        @pl.when(it == GROUP)
         def _():
             weight_step(piece_near, piece_far)
 

time: 221 us -> 222 us (level)
  no operation moved by 1% of the time
where the time goes in v7:
time: 222 us; the launch traced here: 218 us
  Pallas kernels  216 us (97%)
    pallas_call x1, Pallas kernels, layer(): pl.pallas_call(layer_kernel, out_shape=jax.ShapeDtypeStruct((ROWS, D), bf...  216 us

profile of v7, /device:TPU:32, one launch (start us, length us, event | category | flops | bytes accessed | tf_op | source)
XLA Modules:
  0.0 217.7 jit_solution(13329622873742058383)
XLA Ops:
  0.0 215.9 %layer.1 = bf16[48,5120]{1,0:T(8,128)(2,1)} custom-call(bf16[3,48,5120]{2,1,0:T(8,128)(2,1)} %bitcast.4, s32[1,9]{1,0:T(1,128)} %band_ref.1, bf16[40,16,5120]{2,1,0:T(8,128)(2,1)} %bitcast.3, bf16[384,5120]{1,0:T(8,128)(2,1)} %resid_ref.1, f32[4,5120]{1,0:T(4,128)} %modulation_ref.1, bf16[160,864]{1,0:T(8,128)(2,1)} %up_ref.1, bf16[160,864]{1,0:T(8,128)(2,1)} %bitcast.5), custom_call_target="tpu_custom_call" | custom-call | tf_op jit(solution)/shard_map/layer/pallas_call | solution.py:602
  215.9 1.8 copy.9
